TPU v7x, 128 devices: a whole 4x4x4 slice. The times are simulated.
128 devices in a mesh: gx: 16 (over z, y_hi, core), gy: 8 (over x, y_lo).
Axes of the slice: x: 4, y: 4 (y_hi: 2, y_lo: 2; y = y_hi * 2 + y_lo), z: 4, core: 2. Of those that a mesh axis runs over, the one named last changes fastest.
Arguments:
- latent: bfloat16 [16, 8, 4096, 128], P('gx', 'gy'), may hold values from -6 to 6
- edge_state: bfloat16 [16, 8, 16384, 128], P('gx', 'gy'), may hold values from -6 to 6
- w_first: bfloat16 [384, 128], replicated, may hold values from -0.3125 to 0.3125
- w_second: bfloat16 [128, 128], replicated, may hold values from -0.5 to 0.5
- norm_gain: float32 [128], replicated, may hold values from 0.25 to 1.75
- send_list: int32 [16, 8, 4, 128], P('gx', 'gy'), may hold values from 0 to 4095
- send_count: int32 [16, 8, 4], P('gx', 'gy'), may hold values from 0 to 128, as said below
- halo_list: int32 [16, 8, 4, 1024], P('gx', 'gy'), may hold values from 0 to 4095
- senders: int32 [16, 8, 16384], P('gx', 'gy'), may hold values from 0 to 8703, as said below
- receivers: int32 [16, 8, 16384], P('gx', 'gy'), may hold values from 0 to 4607, as said below
- cotangent_edge: bfloat16 [16, 8, 16384, 128], P('gx', 'gy'), may hold values from -6 to 6
- cotangent_agg: bfloat16 [16, 8, 4608, 128], P('gx', 'gy'), may hold values from -6 to 6
Outputs:
- new_edge: bfloat16 [16, 8, 16384, 128], P('gx', 'gy')
- aggregate: bfloat16 [16, 8, 4608, 128], P('gx', 'gy')
- grad_edge: bfloat16 [16, 8, 16384, 128], P('gx', 'gy')
- grad_latent: float32 [16, 8, 4096, 128], P('gx', 'gy')
- grad_first: float32 [384, 128], replicated
- grad_second: float32 [128, 128], replicated
- grad_gain: float32 [128], replicated
Inputs may be any that keep to these rules, and one draw needn't show every extreme that they name: `send_list`: indices into the device's own pre-migration rows. `send_count`: at most 128 particles leave toward one neighbour; some list is full in every draw. `halo_list`: indices into the device's own pre-migration rows. Rows of the device's read table; the 128 edges of each aligned tile have their senders in one aligned block of 128 table rows. Owned rows of the device; the 128 edges of each aligned tile have their receivers in one aligned block of 128 owned rows.
All inputs are finite; a program needn't handle non-finite values.
Results may differ from a plain program's by a relative error of at most 0.0051.
Values may be sent and summed in bfloat16 or wider, within the bound.
A program may use at most 128 MiB of HBM per device.

v0:
```python
import jax
import jax.numpy as jnp
from jax import lax
from jax.sharding import PartitionSpec as P

TILE = 128


eps = 1e-05


def extended(cells, sides, width, closed):
    for axis, dim in sides:
        count = lax.axis_size(axis)
        ends = count if closed else count - 1
        head = lax.slice_in_dim(cells, 0, width, axis=dim)
        tail = lax.slice_in_dim(cells, cells.shape[dim] - width, cells.shape[dim], axis=dim)
        cells = jnp.concatenate(
            [
                lax.ppermute(tail, axis, [(i, (i + 1) % count) for i in range(ends)]),
                cells,
                lax.ppermute(head, axis, [((i + 1) % count, i) for i in range(ends)]),
            ],
            axis=dim,
        )
    return cells


def pick_rows(rows, index, tile_rows):
    width = rows.shape[1]
    blocks = rows.shape[0] // tile_rows
    tiles = index.shape[0] // tile_rows
    grouped = index.reshape(tiles, tile_rows)
    block_id = grouped[:, 0] // tile_rows
    choose = (block_id[:, None] == jnp.arange(blocks, dtype=jnp.int32)[None, :]).astype(
        jnp.bfloat16
    )
    picked = jnp.dot(
        choose, rows.reshape(blocks, tile_rows * width), preferred_element_type=jnp.float32
    )
    picked = picked.astype(jnp.bfloat16).reshape(tiles, tile_rows, width)
    within = (
        (grouped % tile_rows)[:, :, None] == jnp.arange(tile_rows, dtype=jnp.int32)[None, None, :]
    ).astype(jnp.bfloat16)
    result = jnp.einsum("tek,tkd->ted", within, picked, preferred_element_type=jnp.float32)
    return result.astype(jnp.bfloat16).reshape(index.shape[0], width)


def spread_rows(values, index, row_count, tile_rows):
    width = values.shape[1]
    blocks = row_count // tile_rows
    tiles = index.shape[0] // tile_rows
    grouped = index.reshape(tiles, tile_rows)
    block_id = grouped[:, 0] // tile_rows
    within = (
        (grouped % tile_rows)[:, :, None] == jnp.arange(tile_rows, dtype=jnp.int32)[None, None, :]
    ).astype(jnp.float32)
    per_tile = jnp.einsum(
        "tek,ted->tkd",
        within,
        values.reshape(tiles, tile_rows, width),
        precision=lax.Precision.HIGHEST,
        preferred_element_type=jnp.float32,
    )
    choose = (block_id[:, None] == jnp.arange(blocks, dtype=jnp.int32)[None, :]).astype(jnp.float32)
    total = jnp.dot(
        choose.T,
        per_tile.reshape(tiles, tile_rows * width),
        precision=lax.Precision.HIGHEST,
        preferred_element_type=jnp.float32,
    )
    return total.reshape(row_count, width)


def per_device(
    latent,
    edge_state,
    w_first,
    w_second,
    norm_gain,
    send_list,
    send_count,
    halo_list,
    senders,
    receivers,
    cotangent_edge,
    cotangent_agg,
):
    nodes = latent[0, 0]
    edges = edge_state[0, 0]
    send_rows = send_list[0, 0]
    halo_rows = halo_list[0, 0]
    send_idx = senders[0, 0]
    recv_idx = receivers[0, 0]
    cot_edge = cotangent_edge[0, 0]
    cot_agg = cotangent_agg[0, 0]
    part_rows = nodes.shape[0]
    width = nodes.shape[1]
    capacity = send_rows.shape[1]
    boundary = halo_rows.shape[1]
    owned_rows = part_rows + 4 * capacity
    slots = jnp.arange(capacity, dtype=jnp.int32)
    live = slots[None, :] < send_count[0, 0][:, None]
    moved = jnp.where(live[..., None], nodes[send_rows], jnp.zeros((), jnp.bfloat16))
    near = nodes[halo_rows]
    mig_px = extended(moved[0:2].reshape(2 * capacity, width), (("gx", 0),), capacity, True)
    mig_py = extended(moved[2:4].reshape(2 * capacity, width), (("gy", 0),), capacity, False)
    halo_px = extended(near[0:2].reshape(2 * boundary, width), (("gx", 0),), boundary, True)
    halo_py = extended(near[2:4].reshape(2 * boundary, width), (("gy", 0),), boundary, False)
    table = jnp.concatenate(
        [
            nodes,
            mig_px[:capacity],
            mig_px[-capacity:],
            mig_py[:capacity],
            mig_py[-capacity:],
            halo_px[:boundary],
            halo_px[-boundary:],
            halo_py[:boundary],
            halo_py[-boundary:],
        ],
        axis=0,
    )
    table_rows = table.shape[0]
    edge_part = w_first[:width]
    send_part = w_first[width : 2 * width]
    recv_part = w_first[2 * width :]
    send_latent = pick_rows(table, send_idx, TILE)
    recv_latent = pick_rows(table[:owned_rows], recv_idx, TILE)
    preact = (
        jnp.dot(edges, edge_part, preferred_element_type=jnp.float32)
        + jnp.dot(send_latent, send_part, preferred_element_type=jnp.float32)
        + jnp.dot(recv_latent, recv_part, preferred_element_type=jnp.float32)
    )
    hidden = jax.nn.silu(preact).astype(jnp.bfloat16)
    output = jnp.dot(hidden, w_second, preferred_element_type=jnp.float32)
    centred = output - jnp.mean(output, axis=-1, keepdims=True)
    inverse = lax.rsqrt(jnp.mean(centred * centred, axis=-1, keepdims=True) + eps)
    normed = centred * inverse
    message = normed * norm_gain
    new_edge = (edges.astype(jnp.float32) + message).astype(jnp.bfloat16)
    aggregate = spread_rows(message, recv_idx, owned_rows, TILE).astype(jnp.bfloat16)
    d_message = cot_edge.astype(jnp.float32) + pick_rows(cot_agg, recv_idx, TILE).astype(
        jnp.float32
    )
    d_gain = jnp.sum(d_message * normed, axis=0)
    d_norm = d_message * norm_gain
    d_output = (
        inverse
        * (
            d_norm
            - jnp.mean(d_norm, axis=-1, keepdims=True)
            - normed * jnp.mean(d_norm * normed, axis=-1, keepdims=True)
        )
    ).astype(jnp.bfloat16)
    d_second = jnp.dot(hidden.T, d_output, preferred_element_type=jnp.float32)
    d_hidden = jnp.dot(d_output, w_second.T, preferred_element_type=jnp.float32)
    sigmoid_v = jax.nn.sigmoid(preact)
    d_preact = (d_hidden * sigmoid_v * (1.0 + preact * (1.0 - sigmoid_v))).astype(jnp.bfloat16)
    d_first = jnp.concatenate(
        [
            jnp.dot(edges.T, d_preact, preferred_element_type=jnp.float32),
            jnp.dot(send_latent.T, d_preact, preferred_element_type=jnp.float32),
            jnp.dot(recv_latent.T, d_preact, preferred_element_type=jnp.float32),
        ],
        axis=0,
    )
    d_edge = jnp.dot(d_preact, edge_part.T, preferred_element_type=jnp.float32)
    d_send = jnp.dot(d_preact, send_part.T, preferred_element_type=jnp.float32)
    d_recv = jnp.dot(d_preact, recv_part.T, preferred_element_type=jnp.float32)
    grad_edge = (cot_edge.astype(jnp.float32) + d_edge).astype(jnp.bfloat16)
    recv_grad = spread_rows(d_recv, recv_idx, owned_rows, TILE)
    grad_table = spread_rows(d_send, send_idx, table_rows, TILE) + jnp.pad(
        recv_grad, ((0, table_rows - owned_rows), (0, 0))
    )
    summed_first, summed_second, summed_gain = lax.psum((d_first, d_second, d_gain), ("gx", "gy"))
    mig_grad = grad_table[part_rows:owned_rows]
    halo_grad = grad_table[owned_rows:]
    got_mx = extended(
        mig_grad[: 2 * capacity].astype(jnp.bfloat16), (("gx", 0),), capacity, True
    ).astype(jnp.float32)
    got_my = extended(
        mig_grad[2 * capacity :].astype(jnp.bfloat16), (("gy", 0),), capacity, False
    ).astype(jnp.float32)
    got_hx = extended(
        halo_grad[: 2 * boundary].astype(jnp.bfloat16), (("gx", 0),), boundary, True
    ).astype(jnp.float32)
    got_hy = extended(
        halo_grad[2 * boundary :].astype(jnp.bfloat16), (("gy", 0),), boundary, False
    ).astype(jnp.float32)
    back_mig = jnp.stack(
        [got_mx[:capacity], got_mx[-capacity:], got_my[:capacity], got_my[-capacity:]], axis=0
    )
    back_halo = jnp.stack(
        [got_hx[:boundary], got_hx[-boundary:], got_hy[:boundary], got_hy[-boundary:]], axis=0
    )
    back_mig = jnp.where(live[..., None], back_mig, 0.0)
    grad_latent = grad_table[:part_rows]
    grad_latent = grad_latent.at[send_rows.reshape(-1)].add(back_mig.reshape(-1, width))
    grad_latent = grad_latent.at[halo_rows.reshape(-1)].add(back_halo.reshape(-1, width))
    return (
        new_edge[None, None],
        aggregate[None, None],
        grad_edge[None, None],
        grad_latent[None, None],
        summed_first,
        summed_second,
        summed_gain,
    )


def solution(mesh):
    in_specs = (
        P("gx", "gy", None, None),
        P("gx", "gy", None, None),
        P(),
        P(),
        P(),
        P("gx", "gy", None, None),
        P("gx", "gy", None),
        P("gx", "gy", None, None),
        P("gx", "gy", None),
        P("gx", "gy", None),
        P("gx", "gy", None, None),
        P("gx", "gy", None, None),
    )
    out_specs = (
        P("gx", "gy", None, None),
        P("gx", "gy", None, None),
        P("gx", "gy", None, None),
        P("gx", "gy", None, None),
        P(),
        P(),
        P(),
    )
    return jax.shard_map(
        per_device, mesh=mesh, in_specs=in_specs, out_specs=out_specs, check_vma=False
    )
```

profile of v0, /device:TPU:1, one launch (start us, length us, event | category | flops | bytes accessed | tf_op | source)
XLA Modules:
  0.0 400.7 jit_solution(2687549667774742904)
XLA Ops:
  12.5 4.3 %collective-permute-start = (bf16[128,128]{1,0:T(8,128)(2,1)}, bf16[128,128]{1,0:T(8,128)(2,1)}, u32[]{:S(2)}, u32[]{:S(2)}) collective-permute-start(bf16[128,128]{1,0:T(8,128)(2,1)} %get-tuple-element.46), channel_id=1, source_target_pairs={{0,8},{8,16},{16,24},{24,32},{32,40},{40,48},{48,56},{56,64},{64,7... | collective-permute-start | bytes 98312 | tf_op jit(solution)/shard_map/ppermute | solution.py:20
  21.2 12.1 %gather_fusion.1 = bf16[4096,128]{1,0:T(8,128)(2,1)S(1)} fusion(bf16[4096,128]{1,0:T(8,128)(2,1)S(1)} %bitcast.143, s32[4096]{0:T(1024)S(1)} %bitcast_clamp_fusion), kind=kCustom, calls=%fused_computation.1 | custom fusion | bytes 2113536 | tf_op jit(solution)/shard_map/gather | solution.py:105
  34.3 4.1 %collective-permute-start.4 = (bf16[1024,128]{1,0:T(8,128)(2,1)}, bf16[1024,128]{1,0:T(8,128)(2,1)S(1)}, u32[]{:S(2)}, u32[]{:S(2)}) collective-permute-start(bf16[1024,128]{1,0:T(8,128)(2,1)} %get-tuple-element.38), channel_id=1, source_target_pairs={{0,8},{8,16},{16,24},{24,32},{32,40},{40,48},{48,56},{56,64},{64,7... | collective-permute-start | bytes 786440 | tf_op jit(solution)/shard_map/ppermute | solution.py:20
  46.0 4.5 %fusion.24 = f32[16384,128]{1,0:T(8,128)} fusion(bf16[1,1,16384,128]{3,2,1,0:T(8,128)(2,1)S(1)} %copy-done.8, bf16[384,128]{1,0:T(8,128)(2,1)S(1)} %copy-done.16), kind=kOutput, calls=%fused_computation.48 | convolution fusion | flops 536870912 | bytes 12615680 | tf_op jit(solution)/shard_map/dot_general | solution.py:131
  50.5 4.3 %fusion.34 = bf16[128,128,128]{2,1,0:T(8,128)(2,1)} fusion(bf16[128,128,128]{2,1,0:T(8,128)(2,1)S(1)} %bitcast.158, s32[128,128]{1,0:T(8,128)S(1)} %add_select_fusion), kind=kOutput, calls=%fused_computation.58 | convolution fusion | flops 541065216 | bytes 8454144 | tf_op jit(solution)/shard_map/tek,tkd->ted/dot_general | solution.py:45
  56.3 4.7 %collective-permute-start.6 = (bf16[1024,128]{1,0:T(8,128)(2,1)}, bf16[1024,128]{1,0:T(8,128)(2,1)}, u32[]{:S(2)}, u32[]{:S(2)}) collective-permute-start(bf16[1024,128]{1,0:T(8,128)(2,1)} %get-tuple-element.36), channel_id=1, source_target_pairs={{0,1},{1,2},{2,3},{3,4},{4,5},{5,6},{6,7},{8,9},{9,10},{10,11},{11... | collective-permute-start | bytes 786440 | tf_op jit(solution)/shard_map/ppermute | solution.py:20
  67.7 4.4 %fusion.33 = bf16[128,128,128]{2,1,0:T(8,128)(2,1)} fusion(bf16[128,128,128]{2,1,0:T(8,128)(2,1)S(1)} %bitcast.159, s32[128,128]{1,0:T(8,128)S(1)} %add_select_fusion), kind=kOutput, calls=%fused_computation.57 | convolution fusion | flops 541065216 | bytes 8454144 | tf_op jit(solution)/shard_map/tek,tkd->ted/dot_general | solution.py:45
  77.8 4.8 %reshape.297 = bf16[68,16384]{1,0:T(8,128)(2,1)} reshape(bf16[8704,128]{1,0:T(8,128)(2,1)} %constant_dynamic-update-slice_fusion) | data formatting | bytes 4456448 | tf_op jit(solution)/shard_map/reshape | solution.py:39
  82.6 3.0 fusion.35
  91.5 4.5 %multiply_convert_fusion.1 = (bf16[16384,128]{1,0:T(8,128)(2,1)S(1)}, f32[16384,128]{1,0:T(8,128)}) fusion(f32[16384,128]{1,0:T(8,128)S(1)} %convolution_add_fusion.2, bf16[16384,128]{1,0:T(8,128)(2,1)S(1)} %bitcast.150, bf16[384,128]{1,0:T(8,128)(2,1)S(1)} %copy-done.16), kind=kOutput, calls=%fused_computation.30 | convolution fusion | flops 549453824 | bytes 25198592 | tf_op jit(solution)/shard_map/dot_general | solution.py:133
  98.4 4.9 %multiply_reduce_fusion.2 = f32[16384]{0:T(1024)S(1)} fusion(f32[16384,128]{1,0:T(8,128)S(1)} %get-tuple-element.60, f32[16384]{0:T(1024)S(1)} %broadcast_multiply_fusion.2), kind=kLoop, calls=%fused_computation.29 | loop fusion | flops 6275072 | bytes 8519680 | tf_op jit(solution)/shard_map/reduce_sum | solution.py:138
  103.4 9.9 %multiply_reduce_fusion = (f32[128]{0:T(128)S(1)}, f32[16384]{0:T(1024)S(1)}, f32[16384]{0:T(1024)S(1)}) fusion(f32[16384,128]{1,0:T(8,128)S(1)} %get-tuple-element.60, bf16[128,128,128]{2,1,0:T(8,128)(2,1)S(1)} %copy-done.10, bf16[1,1,16384,128]{3,2,1,0:T(8,128)(2,1)S(1)} %copy-done.6, f32[16384]{0:T(1024)S(1)} %add_rsqrt_fusion, ...), kind=kLoop, calls=%fused_computation.25 | loop fusion | flops 23035776 | bytes 17040384 | tf_op jit(solution)/shard_map/reduce_sum | solution.py:146
  113.4 15.6 %fusion.21 = (bf16[1,1,16384,128]{3,2,1,0:T(8,128)(2,1)}, f32[16384,128]{1,0:T(8,128)}, bf16[16384,128]{1,0:T(8,128)(2,1)}) fusion(bf16[1,1,16384,128]{3,2,1,0:T(8,128)(2,1)S(1)} %copy-done.9, f32[128]{0:T(128)S(1)} %copy-done.23, f32[16384]{0:T(1024)S(1)} %add_rsqrt_fusion, f32[16384,128]{1,0:T(8,128)S(1)} %get-tuple-element.60, ...), kind=kLoop, calls=%fused_computation.45 | loop fusion | flops 31457280 | bytes 38011392 | tf_op jit(solution)/shard_map/broadcast_in_dim | solution.py:202
  129.0 8.7 %fusion.1 = bf16[16384,128]{1,0:T(8,128)(2,1)S(1)} fusion(bf16[16384,128]{1,0:T(8,128)(2,1)} %get-tuple-element.16, bf16[128,128]{1,0:T(8,128)(2,1)S(1)} %copy-done, f32[16384,128]{1,0:T(8,128)} %get-tuple-element.58), kind=kOutput, calls=%fused_computation.9 | convolution fusion | flops 555745280 | bytes 16809984 | tf_op jit(solution)/shard_map/dot_general | solution.py:157
  148.1 4.5 %fusion.49 = f32[16384,128]{1,0:T(8,128)} fusion(bf16[16384,128]{1,0:T(8,128)(2,1)S(1)} %fusion.1, bf16[384,128]{1,0:T(8,128)(2,1)S(1)} %copy-done.16), kind=kOutput, calls=%fused_computation.110 | convolution fusion | flops 536870912 | bytes 12615680 | tf_op jit(solution)/shard_map/dot_general | solution.py:170
  152.6 6.6 %fusion.16 = f32[128,128,128]{2,1,0:T(8,128)S(1)} fusion(f32[128,128,128]{2,1,0:T(8,128)S(1)} %bitcast.149, s32[128,128]{1,0:T(8,128)S(1)} %add_select_fusion.1), kind=kOutput, calls=%fused_computation.38 | convolution fusion | flops 3223322624 | bytes 16842752 | tf_op jit(solution)/shard_map/tek,ted->tkd/dot_general | solution.py:58
  159.1 12.0 %fusion.7 = f32[68,16384]{1,0:T(8,128)} fusion(f32[16,8,128,128]{3,2,1,0:T(8,128)S(1)} %bitcast.155, s32[128]{0:T(128)S(1)} %fusion.60), kind=kOutput, calls=%fused_computation.20 | convolution fusion | flops 1711284736 | bytes 12845568 | tf_op jit(solution)/shard_map/dot_general | solution.py:66
  171.2 5.9 %reshape.308 = f32[8704,128]{1,0:T(8,128)} reshape(f32[68,16384]{1,0:T(8,128)} %fusion.7) | data formatting | bytes 8912896 | tf_op jit(solution)/shard_map/reshape | solution.py:72
  177.1 8.4 %fusion.12 = f32[128,128,128]{2,1,0:T(8,128)S(1)} fusion(f32[128,128,128]{2,1,0:T(8,128)} %bitcast.148, s32[128,128]{1,0:T(8,128)S(1)} %add_select_fusion), kind=kOutput, calls=%fused_computation.33 | convolution fusion | flops 3223322624 | bytes 16842752 | tf_op jit(solution)/shard_map/tek,ted->tkd/dot_general | solution.py:58
  185.5 9.5 %fusion.4 = f32[36,16384]{1,0:T(8,128)} fusion(f32[16,8,128,128]{3,2,1,0:T(8,128)S(1)} %bitcast.157, s32[128]{0:T(128)S(1)} %fusion.59), kind=kOutput, calls=%fused_computation.17 | convolution fusion | flops 905974272 | bytes 10748416 | tf_op jit(solution)/shard_map/dot_general | solution.py:66
  195.0 3.7 reshape.311
  198.7 5.3 %fusion.62 = (bf16[8704,128]{1,0:T(8,128)(2,1)S(1)}, f32[8704,128]{1,0:T(8,128)}) fusion(f32[8704,128]{1,0:T(8,128)} %reshape.308, f32[4608,128]{1,0:T(8,128)} %reshape.311), kind=kLoop, calls=%fused_computation.150 | loop fusion | flops 2228224 | bytes 13500416 | tf_op jit(solution)/shard_map/convert.5
  207.3 3.3 fusion.3
  210.6 3.8 collective-permute-start.12
  216.3 5.2 %collective-permute-start.14 = (bf16[1024,128]{1,0:T(8,128)(2,1)}, bf16[1024,128]{1,0:T(8,128)(2,1)}, u32[]{:S(2)}, u32[]{:S(2)}) collective-permute-start(bf16[1024,128]{1,0:T(8,128)(2,1)} %get-tuple-element.19), channel_id=1, source_target_pairs={{0,1},{1,2},{2,3},{3,4},{4,5},{5,6},{6,7},{8,9},{9,10},{10,11},{11... | collective-permute-start | bytes 786440 | tf_op jit(solution)/shard_map/ppermute | solution.py:20
  223.0 4.5 %collective-permute-start.9 = (bf16[128,128]{1,0:T(8,128)(2,1)}, bf16[128,128]{1,0:T(8,128)(2,1)}, u32[]{:S(2)}, u32[]{:S(2)}) collective-permute-start(bf16[128,128]{1,0:T(8,128)(2,1)} %get-tuple-element.26), channel_id=1, source_target_pairs={{8,0},{16,8},{24,16},{32,24},{40,32},{48,40},{56,48},{64,56},{72,6... | collective-permute-start | bytes 98312 | tf_op jit(solution)/shard_map/ppermute | solution.py:22
  227.5 6.2 %fusion.14 = f32[128,128,128]{2,1,0:T(8,128)S(1)} fusion(f32[128,128,128]{2,1,0:T(8,128)S(1)} %bitcast.154, s32[128,128]{1,0:T(8,128)S(1)} %add_select_fusion), kind=kOutput, calls=%fused_computation.35 | convolution fusion | flops 3223322624 | bytes 16842752 | tf_op jit(solution)/shard_map/tek,ted->tkd/dot_general | solution.py:58
  233.7 8.3 %convolution_convert_fusion.3 = bf16[36,16384]{1,0:T(8,128)(2,1)S(1)} fusion(f32[16,8,128,128]{3,2,1,0:T(8,128)S(1)} %bitcast.156, s32[128]{0:T(128)S(1)} %fusion.59), kind=kOutput, calls=%fused_computation.15 | convolution fusion | flops 906564096 | bytes 9568768 | tf_op jit(solution)/shard_map/dot_general | solution.py:66
  246.1 67.8 %psum.23 = f32[128]{0:T(128)} all-reduce(f32[128]{0:T(128)S(1)} %get-tuple-element.7), channel_id=1, replica_groups=mesh['gx'=16,'gy'=8] {'gx','gy'}, use_global_device_ids=true, to_apply=%region_9.10 | all-reduce | flops 128 | bytes 1024 | tf_op jit(solution)/shard_map/psum | solution.py:176
  321.6 4.1 %scatter_fusion = f32[4096,128]{1,0:T(8,128)S(1)} fusion(f32[4096,128]{1,0:T(8,128)S(1)} %slice.222, s32[512]{0:T(512)S(1)} %bitcast.169, f32[512,128]{1,0:T(8,128)S(1)} %bitcast_select_fusion), kind=kCustom, calls=%fused_computation.2 | custom fusion | flops 65536 | bytes 788480 | tf_op jit(solution)/shard_map/scatter-add | solution.py:199
  330.7 23.4 %scatter_fusion.1 = f32[4096,128]{1,0:T(8,128)S(1)} fusion(f32[4096,128]{1,0:T(8,128)S(1)} %scatter_fusion, s32[4096]{0:T(1024)S(1)} %bitcast.167, f32[4096,128]{1,0:T(8,128)} %bitcast.161), kind=kCustom, calls=%fused_computation.3 | custom fusion | flops 524288 | bytes 6307840 | tf_op jit(solution)/shard_map/scatter-add | solution.py:200
  354.2 36.4 %all-reduce.4.cloned.1.call-done = (f32[384,128]{1,0:T(8,128)}, f32[128,128]{1,0:T(8,128)}) async-done(((f32[384,128]{1,0:T(8,128)}, f32[128,128]{1,0:T(8,128)}), (f32[384,128]{1,0:T(8,128)}, f32[128,128]{1,0:T(8,128)})) %all-reduce.4.cloned.1.call-update) | async-done | bytes 262160 | tf_op jit(solution)/shard_map/psum | solution.py:176
  (149 shorter events, 77.2 us)
Async XLA Ops:
  7.2 88.8 %copy-start = (bf16[128,128]{1,0:T(8,128)(2,1)S(1)}, bf16[128,128]{1,0:T(8,128)(2,1)}, u32[]{:S(2)}) copy-start(bf16[128,128]{1,0:T(8,128)(2,1)} %param.15) | copy-start | bytes 98308
  7.2 14.0 %copy-start.5 = (bf16[1,1,4096,128]{3,2,1,0:T(8,128)(2,1)S(1)}, bf16[1,1,4096,128]{3,2,1,0:T(8,128)(2,1)}, u32[]{:S(2)}) copy-start(bf16[1,1,4096,128]{3,2,1,0:T(8,128)(2,1)} %param.12) | copy-start | bytes 3145732
  7.2 383.4 %all-reduce.4.cloned.1.call-start = ((), (), s32[]{:S(2)}) async-start(), calls=%async_computation | async-start | bytes 524288 | tf_op jit(solution)/shard_map/psum | solution.py:176
  12.5 42.3 %collective-permute-start = (bf16[128,128]{1,0:T(8,128)(2,1)}, bf16[128,128]{1,0:T(8,128)(2,1)}, u32[]{:S(2)}, u32[]{:S(2)}) collective-permute-start(bf16[128,128]{1,0:T(8,128)(2,1)} %get-tuple-element.46), channel_id=1, source_target_pairs={{0,8},{8,16},{16,24},{24,32},{32,40},{40,48},{48,56},{56,64},{64,7... | collective-permute-start | bytes 98312 | tf_op jit(solution)/shard_map/ppermute | solution.py:20
  16.8 39.5 %collective-permute-start.1 = (bf16[128,128]{1,0:T(8,128)(2,1)}, bf16[128,128]{1,0:T(8,128)(2,1)S(1)}, u32[]{:S(2)}, u32[]{:S(2)}) collective-permute-start(bf16[128,128]{1,0:T(8,128)(2,1)} %get-tuple-element.45), channel_id=1, source_target_pairs={{8,0},{16,8},{24,16},{32,24},{40,32},{48,40},{56,48},{64,56},{72,6... | collective-permute-start | bytes 98312 | tf_op jit(solution)/shard_map/ppermute | solution.py:22
  16.8 44.7 %collective-permute-start.2 = (bf16[128,128]{1,0:T(8,128)(2,1)}, bf16[128,128]{1,0:T(8,128)(2,1)S(1)}, u32[]{:S(2)}, u32[]{:S(2)}) collective-permute-start(bf16[128,128]{1,0:T(8,128)(2,1)} %get-tuple-element.44), channel_id=1, source_target_pairs={{0,1},{1,2},{2,3},{3,4},{4,5},{5,6},{6,7},{8,9},{9,10},{10,11},{11... | collective-permute-start | bytes 98312 | tf_op jit(solution)/shard_map/ppermute | solution.py:20
  19.1 44.8 %collective-permute-start.3 = (bf16[128,128]{1,0:T(8,128)(2,1)}, bf16[128,128]{1,0:T(8,128)(2,1)S(1)}, u32[]{:S(2)}, u32[]{:S(2)}) collective-permute-start(bf16[128,128]{1,0:T(8,128)(2,1)} %get-tuple-element.43), channel_id=1, source_target_pairs={{1,0},{2,1},{3,2},{4,3},{5,4},{6,5},{7,6},{9,8},{10,9},{11,10},{12... | collective-permute-start | bytes 98312 | tf_op jit(solution)/shard_map/ppermute | solution.py:22
  33.3 6.3 %copy-start.17 = (s32[1,1,16384]{2,1,0:T(1,128)S(1)}, s32[1,1,16384]{2,1,0:T(1,128)}, u32[]{:S(2)}) copy-start(s32[1,1,16384]{2,1,0:T(1,128)} %param.20) | copy-start | bytes 196612
  33.3 6.4 %copy-start.18 = (s32[1,1,16384]{2,1,0:T(1,128)S(1)}, s32[1,1,16384]{2,1,0:T(1,128)}, u32[]{:S(2)}) copy-start(s32[1,1,16384]{2,1,0:T(1,128)} %param.21) | copy-start | bytes 196612
  34.3 37.7 %collective-permute-start.4 = (bf16[1024,128]{1,0:T(8,128)(2,1)}, bf16[1024,128]{1,0:T(8,128)(2,1)S(1)}, u32[]{:S(2)}, u32[]{:S(2)}) collective-permute-start(bf16[1024,128]{1,0:T(8,128)(2,1)} %get-tuple-element.38), channel_id=1, source_target_pairs={{0,8},{8,16},{16,24},{24,32},{32,40},{40,48},{48,56},{56,64},{64,7... | collective-permute-start | bytes 786440 | tf_op jit(solution)/shard_map/ppermute | solution.py:20
  54.8 18.0 %collective-permute-start.5 = (bf16[1024,128]{1,0:T(8,128)(2,1)}, bf16[1024,128]{1,0:T(8,128)(2,1)}, u32[]{:S(2)}, u32[]{:S(2)}) collective-permute-start(bf16[1024,128]{1,0:T(8,128)(2,1)} %get-tuple-element.37), channel_id=1, source_target_pairs={{8,0},{16,8},{24,16},{32,24},{40,32},{48,40},{56,48},{64,56},{72,6... | collective-permute-start | bytes 786440 | tf_op jit(solution)/shard_map/ppermute | solution.py:22
  56.3 18.2 %collective-permute-start.6 = (bf16[1024,128]{1,0:T(8,128)(2,1)}, bf16[1024,128]{1,0:T(8,128)(2,1)}, u32[]{:S(2)}, u32[]{:S(2)}) collective-permute-start(bf16[1024,128]{1,0:T(8,128)(2,1)} %get-tuple-element.36), channel_id=1, source_target_pairs={{0,1},{1,2},{2,3},{3,4},{4,5},{5,6},{6,7},{8,9},{9,10},{10,11},{11... | collective-permute-start | bytes 786440 | tf_op jit(solution)/shard_map/ppermute | solution.py:20
  61.6 14.6 %collective-permute-start.7 = (bf16[1024,128]{1,0:T(8,128)(2,1)}, bf16[1024,128]{1,0:T(8,128)(2,1)}, u32[]{:S(2)}, u32[]{:S(2)}) collective-permute-start(bf16[1024,128]{1,0:T(8,128)(2,1)} %get-tuple-element.35), channel_id=1, source_target_pairs={{1,0},{2,1},{3,2},{4,3},{5,4},{6,5},{7,6},{9,8},{10,9},{11,10},{12... | collective-permute-start | bytes 786440 | tf_op jit(solution)/shard_map/ppermute | solution.py:22
  103.4 10.0 %copy-start.9 = (bf16[1,1,16384,128]{3,2,1,0:T(8,128)(2,1)S(1)}, bf16[1,1,16384,128]{3,2,1,0:T(8,128)(2,1)}, u32[]{:S(2)}) copy-start(bf16[1,1,16384,128]{3,2,1,0:T(8,128)(2,1)} %param.13) | copy-start | bytes 12582916
  137.7 10.4 %copy-start.2 = (bf16[16384,128]{1,0:T(8,128)(2,1)}, bf16[16384,128]{1,0:T(8,128)(2,1)S(1)}, u32[]{:S(2)}) copy-start(bf16[16384,128]{1,0:T(8,128)(2,1)S(1)} %fusion.1) | copy-start | bytes 12582916
  198.7 8.6 %copy-start.7 = (bf16[1,1,16384,128]{3,2,1,0:T(8,128)(2,1)S(1)}, bf16[1,1,16384,128]{3,2,1,0:T(8,128)(2,1)}, u32[]{:S(2)}) copy-start(bf16[1,1,16384,128]{3,2,1,0:T(8,128)(2,1)} %param.22) | copy-start | bytes 12582916
  206.7 20.8 %slice-start.2 = ((s8[8388608]{0:T(1024)(128)(4,1)}), s8[4194304]{0:T(1024)(128)(4,1)S(1)}, s32[]{:S(2)}) async-start(s8[8388608]{0:T(1024)(128)(4,1)} %bitcast.152), calls=%async_computation.3 | async-start | bytes 8388608
  207.3 20.2 %slice-start.3 = ((s8[8388608]{0:T(1024)(128)(4,1)}), s8[4194304]{0:T(1024)(128)(4,1)S(1)}, s32[]{:S(2)}) async-start(s8[8388608]{0:T(1024)(128)(4,1)} %bitcast.152), calls=%async_computation.4 | async-start | bytes 8388608
  210.6 115.0 %collective-permute-start.12 = (bf16[1024,128]{1,0:T(8,128)(2,1)}, bf16[1024,128]{1,0:T(8,128)(2,1)}, u32[]{:S(2)}, u32[]{:S(2)}) collective-permute-start(bf16[1024,128]{1,0:T(8,128)(2,1)} %get-tuple-element.17), channel_id=1, source_target_pairs={{0,8},{8,16},{16,24},{24,32},{32,40},{40,48},{48,56},{56,64},{64,7... | collective-permute-start | bytes 786440 | tf_op jit(solution)/shard_map/ppermute | solution.py:20
  214.5 111.2 %collective-permute-start.13 = (bf16[1024,128]{1,0:T(8,128)(2,1)}, bf16[1024,128]{1,0:T(8,128)(2,1)}, u32[]{:S(2)}, u32[]{:S(2)}) collective-permute-start(bf16[1024,128]{1,0:T(8,128)(2,1)} %get-tuple-element.20), channel_id=1, source_target_pairs={{8,0},{16,8},{24,16},{32,24},{40,32},{48,40},{56,48},{64,56},{72,6... | collective-permute-start | bytes 786440 | tf_op jit(solution)/shard_map/ppermute | solution.py:22
  216.3 110.5 %collective-permute-start.14 = (bf16[1024,128]{1,0:T(8,128)(2,1)}, bf16[1024,128]{1,0:T(8,128)(2,1)}, u32[]{:S(2)}, u32[]{:S(2)}) collective-permute-start(bf16[1024,128]{1,0:T(8,128)(2,1)} %get-tuple-element.19), channel_id=1, source_target_pairs={{0,1},{1,2},{2,3},{3,4},{4,5},{5,6},{6,7},{8,9},{9,10},{10,11},{11... | collective-permute-start | bytes 786440 | tf_op jit(solution)/shard_map/ppermute | solution.py:20
  221.5 92.4 %collective-permute-start.8 = (bf16[128,128]{1,0:T(8,128)(2,1)}, bf16[128,128]{1,0:T(8,128)(2,1)}, u32[]{:S(2)}, u32[]{:S(2)}) collective-permute-start(bf16[128,128]{1,0:T(8,128)(2,1)} %get-tuple-element.23), channel_id=1, source_target_pairs={{0,8},{8,16},{16,24},{24,32},{32,40},{40,48},{48,56},{56,64},{64,7... | collective-permute-start | bytes 98312 | tf_op jit(solution)/shard_map/ppermute | solution.py:20
  223.0 93.7 %collective-permute-start.9 = (bf16[128,128]{1,0:T(8,128)(2,1)}, bf16[128,128]{1,0:T(8,128)(2,1)}, u32[]{:S(2)}, u32[]{:S(2)}) collective-permute-start(bf16[128,128]{1,0:T(8,128)(2,1)} %get-tuple-element.26), channel_id=1, source_target_pairs={{8,0},{16,8},{24,16},{32,24},{40,32},{48,40},{56,48},{64,56},{72,6... | collective-permute-start | bytes 98312 | tf_op jit(solution)/shard_map/ppermute | solution.py:22
  241.9 79.5 %copy-start.24 = (pred[512]{0:T(512)(128)(4,1)S(1)}, pred[512]{0:T(512)(128)(4,1)}, u32[]{:S(2)}) copy-start(pred[512]{0:T(512)(128)(4,1)} %get-tuple-element.55) | copy-start | bytes 1540
  242.6 79.0 %copy-start.21 = (s32[512,1]{0,1:T(1,128)S(1)}, s32[512,1]{0,1:T(1,128)}, u32[]{:S(2)}) copy-start(s32[512,1]{0,1:T(1,128)} %compare_select_fusion.2) | copy-start | bytes 6148
  246.0 79.6 %copy-start.15 = (bf16[2048,128]{1,0:T(8,128)(2,1)S(1)}, bf16[2048,128]{1,0:T(8,128)(2,1)}, u32[]{:S(2)}) copy-start(bf16[2048,128]{1,0:T(8,128)(2,1)} %get-tuple-element.21) | copy-start | bytes 1572868
  246.0 82.1 %copy-start.14 = (bf16[2048,128]{1,0:T(8,128)(2,1)S(1)}, bf16[2048,128]{1,0:T(8,128)(2,1)}, u32[]{:S(2)}) copy-start(bf16[2048,128]{1,0:T(8,128)(2,1)} %get-tuple-element.22) | copy-start | bytes 1572868
  313.9 5.0 %collective-permute-start.10 = (bf16[128,128]{1,0:T(8,128)(2,1)S(1)}, bf16[128,128]{1,0:T(8,128)(2,1)S(1)}, u32[]{:S(2)}, u32[]{:S(2)}) collective-permute-start(bf16[128,128]{1,0:T(8,128)(2,1)S(1)} %get-tuple-element.25), channel_id=1, source_target_pairs={{0,1},{1,2},{2,3},{3,4},{4,5},{5,6},{6,7},{8,9},{9,10},{10,11},{11... | collective-permute-start | bytes 98312 | tf_op jit(solution)/shard_map/ppermute | solution.py:20
  316.7 4.7 %collective-permute-start.11 = (bf16[128,128]{1,0:T(8,128)(2,1)S(1)}, bf16[128,128]{1,0:T(8,128)(2,1)S(1)}, u32[]{:S(2)}, u32[]{:S(2)}) collective-permute-start(bf16[128,128]{1,0:T(8,128)(2,1)S(1)} %get-tuple-element.24), channel_id=1, source_target_pairs={{1,0},{2,1},{3,2},{4,3},{5,4},{6,5},{7,6},{9,8},{10,9},{11,10},{12... | collective-permute-start | bytes 98312 | tf_op jit(solution)/shard_map/ppermute | solution.py:22
  318.8 9.3 %collective-permute-start.15 = (bf16[1024,128]{1,0:T(8,128)(2,1)}, bf16[1024,128]{1,0:T(8,128)(2,1)}, u32[]{:S(2)}, u32[]{:S(2)}) collective-permute-start(bf16[1024,128]{1,0:T(8,128)(2,1)} %get-tuple-element.18), channel_id=1, source_target_pairs={{1,0},{2,1},{3,2},{4,3},{5,4},{6,5},{7,6},{9,8},{10,9},{11,10},{12... | collective-permute-start | bytes 786440 | tf_op jit(solution)/shard_map/ppermute | solution.py:22
  330.7 62.9 %copy-start.1 = (bf16[128,128]{1,0:T(8,128)(2,1)S(1)}, bf16[128,128]{1,0:T(8,128)(2,1)}, u32[]{:S(2)}) copy-start(bf16[128,128]{1,0:T(8,128)(2,1)} %param.15) | copy-start | bytes 98308
  354.2 39.5 %copy-start.4 = (f32[4096,128]{1,0:T(8,128)}, f32[4096,128]{1,0:T(8,128)S(1)}, u32[]{:S(2)}) copy-start(f32[4096,128]{1,0:T(8,128)S(1)} %scatter_fusion.1) | copy-start | bytes 6291460
  (14 other events, 49.9 us)
Sparse Core Ops, SparseCore 0:
  246.2 144.3 all-reduce.3
where the time goes:
time: 408 us; the launch traced here: 401 us
  matrix products  104 us (25%)
  other arithmetic  72.8 us (18%)
  blocking collectives  67.8 us (17%)
  local copies, waits for them, and re-layouts  61.5 us (15%)
  starting transfers between devices  40.8 us (10%)
  waiting for transfers between devices  39.1 us (10%)
  between operations  14.9 us (4%)
    psum x1, blocking collectives, per_device(): lax.psum((d_first, d_second, d_gain), ('gx', 'gy'))  67.8 us
    psum x1, waiting for transfers between devices, per_device(): lax.psum((d_first, d_second, d_gain), ('gx', 'gy'))  36.4 us
    dot_general x3, matrix products, spread_rows(): jnp.dot(choose.T, per_tile.reshape(tiles, tile_rows * width), precision=l...  29.8 us
    ppermute x8, starting transfers between devices, extended(): lax.ppermute(tail, axis, [(i, (i + 1) % count) for i in range(ends)])  28.7 us
    scatter-add x1, other arithmetic, per_device(): grad_latent.at[halo_rows.reshape(-1)].add(back_halo.reshape(-1, width))  23.4 us
    dot_general x3, matrix products, spread_rows(): jnp.einsum('tek,ted->tkd', within, values.reshape(tiles, tile_rows, width...  21.1 us
    unnamed x73, local copies, waits for them, and re-layouts  19 us
    broadcast_in_dim x1, other arithmetic, per_device(): new_edge[None, None]  15.6 us
  transfers between devices with their start and end apart: 17, of which 3 were waited for; matrix products, arithmetic and copies ran while one was open for 24% of the time, Pallas kernels for 0%

commit v1 on v0

v1 whole, which is shorter than its diff:
```python
import functools

import jax
import jax.numpy as jnp
from jax import lax
from jax.experimental import pallas as pl
from jax.experimental.pallas import tpu as pltpu
from jax.sharding import PartitionSpec as P

MESH = pl.DeviceIdType.MESH
F32 = jnp.float32
BF16 = jnp.bfloat16
TILE = 128
EPS = 1e-05
N_GX = 16
N_GY = 8
OWN_BLOCKS = 32
MIG_BLOCKS = 4
HALO_BLOCKS = 32
OWNED_BLOCKS = OWN_BLOCKS + MIG_BLOCKS
FAR_BLOCKS = MIG_BLOCKS + HALO_BLOCKS
TABLE_BLOCKS = OWN_BLOCKS + FAR_BLOCKS
PER_DIR = HALO_BLOCKS // 4
HALF = OWN_BLOCKS * TILE // 2
PAIRS = 4
RANKS = 32
CHUNK = 24
VMEM_LIMIT = 62 * 2**20
WEIGHT_CHUNK = 16


def mm(a, b):
    return jnp.dot(a, b, preferred_element_type=F32)


def mmt(a, b):
    return lax.dot_general(a, b, (((1,), (1,)), ((), ())), preferred_element_type=F32)


def onehot(rows, row_index, base):
    lanes = row_index.shape[1]
    row = lax.broadcasted_iota(jnp.int16, (rows, lanes), 0)
    index = jnp.broadcast_to((row_index - base).astype(jnp.int16), (rows, lanes))
    return jnp.where(row == index, jnp.ones((), BF16), jnp.zeros((), BF16))


def neighbour(k):
    i = lax.axis_index("gx")
    j = lax.axis_index("gy")
    if k == 0:
        return (lax.rem(i + N_GX - 1, N_GX), j), None
    if k == 1:
        return (lax.rem(i + 1, N_GX), j), None
    if k == 2:
        return (i, j - 1), j > 0
    return (i, j + 1), j < N_GY - 1


def guarded(exists, action):
    if exists is None:
        action()
    else:
        pl.when(exists)(action)


def greet_neighbours(barrier):
    for k in range(4):
        device, exists = neighbour(k)

        def signal(device=device):
            pl.semaphore_signal(barrier, inc=1, device_id=device, device_id_type=MESH)

        guarded(exists, signal)


def neighbour_count():
    j = lax.axis_index("gy")
    return 2 + jnp.where(j > 0, 1, 0) + jnp.where(j < N_GY - 1, 1, 0)


HALO_RUN = 4
RUNS = [(0, 1)] + [(1 + at, HALO_RUN) for at in range(0, PER_DIR, HALO_RUN)]


def table_place(direction, at):
    if at == 0:
        return direction
    return MIG_BLOCKS + direction * PER_DIR + at - 1


def far_copy(src, dst, send_sem, recv_sem, k, run, base, to_slot):
    at, count = RUNS[run]
    device, exists = neighbour(k)
    copy = pltpu.make_async_remote_copy(
        src_ref=src.at[pl.ds(table_place(k, at), count)],
        dst_ref=dst.at[pl.ds(base + table_place(to_slot, at), count)],
        send_sem=send_sem.at[k, run],
        recv_sem=recv_sem.at[to_slot, run],
        device_id=device,
        device_id_type=MESH,
    )
    return copy, exists


def fetch_kernel(
    lat_ref, send_ref, count_ref, halo_ref, snd_ref, rcv_ref,
    tab_ref, meta_ref,
    lat_t, out_buf, zero_buf, send_sem, recv_sem, own_sem, zero_sem,
):
    barrier = pltpu.get_barrier_semaphore()
    greet_neighbours(barrier)

    def turn(b, _):
        rows = lat_ref[pl.ds(pl.multiple_of(b * TILE, TILE), TILE), :]
        lat_t[b] = rows.T
        return 0

    lax.fori_loop(0, OWN_BLOCKS, turn, 0, unroll=4)
    own_copy = pltpu.make_async_copy(lat_t, tab_ref.at[pl.ds(0, OWN_BLOCKS)], own_sem)
    own_copy.start()
    zero_buf[...] = jnp.zeros_like(zero_buf)
    half = OWN_BLOCKS // 2

    def zero_copies(k):
        return [
            pltpu.make_async_copy(
                zero_buf.at[pl.ds(0, count)],
                tab_ref.at[pl.ds(OWN_BLOCKS + table_place(k, at), count)],
                zero_sem.at[k, run],
            )
            for run, (at, count) in enumerate(RUNS)
        ]

    for k in (2, 3):
        _, exists = neighbour(k)

        def fill(k=k):
            for copy in zero_copies(k):
                copy.start()

        pl.when(jnp.logical_not(exists))(fill)

    def pick(index):
        low = jnp.where(index >= HALF, index - HALF, index)
        acc = None
        for piece in range(half // 2):
            hot = onehot(2 * TILE, low, piece * 2 * TILE)
            left = jnp.concatenate(
                [
                    jnp.concatenate([lat_t[2 * piece], lat_t[2 * piece + 1]], axis=1),
                    jnp.concatenate([lat_t[half + 2 * piece], lat_t[half + 2 * piece + 1]], axis=1),
                ],
                axis=0,
            )
            part = mm(left, hot)
            acc = part if acc is None else acc + part
        upper = jnp.broadcast_to(index >= HALF, (TILE, index.shape[1]))
        return jnp.where(upper, acc[TILE:], acc[:TILE]).astype(BF16)

    slot = lax.broadcasted_iota(jnp.int32, (1, TILE), 1)

    def live_index(k):
        return jnp.where(slot < count_ref[k], send_ref[pl.ds(k, 1), :], -1)

    for pair in range(2):
        index = jnp.concatenate([live_index(2 * pair), live_index(2 * pair + 1)], axis=1)
        rows = pick(index)
        out_buf[2 * pair] = rows[:, :TILE]
        out_buf[2 * pair + 1] = rows[:, TILE:]

    pl.semaphore_wait(barrier, neighbour_count())

    def start(k, run):
        copy, exists = far_copy(out_buf, tab_ref, send_sem, recv_sem, k, run, OWN_BLOCKS, k ^ 1)
        guarded(exists, copy.start)

    for k in (2, 3, 0, 1):
        start(k, 0)
    for run in range(1, len(RUNS)):
        at, count = RUNS[run]
        for k in (2, 3, 0, 1):

            def gather(step, _, k=k, at=at):
                first = pl.multiple_of((at - 1) * TILE + step * 2 * TILE, 2 * TILE)
                rows = pick(halo_ref[pl.ds(k, 1), pl.ds(first, 2 * TILE)])
                place = table_place(k, at) + 2 * step
                out_buf[place] = rows[:, :TILE]
                out_buf[place + 1] = rows[:, TILE:]
                return 0

            lax.fori_loop(0, count // 2, gather, 0)
            start(k, run)

    firsts = lax.shift_right_logical(
        jnp.concatenate([snd_ref[...].T[:1], rcv_ref[...].T[:1]], axis=0), 7
    )
    meta_ref[...] = firsts

    own_copy.wait()
    for k in (2, 3):
        _, exists = neighbour(k)

        def drain(k=k):
            for copy in zero_copies(k):
                copy.wait()

        pl.when(jnp.logical_not(exists))(drain)
    for run in range(len(RUNS)):
        for k in range(4):
            copy, exists = far_copy(
                out_buf, tab_ref, send_sem, recv_sem, k, run, OWN_BLOCKS, k ^ 1
            )
            guarded(exists, copy.wait_send)
            back, exists = far_copy(out_buf, tab_ref, send_sem, recv_sem, k, run, OWN_BLOCKS, k)
            guarded(exists, back.wait_recv)


def fetch(nodes, send_rows, counts, halo_rows, send_idx, recv_idx):
    vmem = pl.BlockSpec(memory_space=pltpu.VMEM)
    smem = pl.BlockSpec(memory_space=pltpu.SMEM)
    block = (TILE, TILE)
    return pl.pallas_call(
        fetch_kernel,
        name="fetch_rows",
        out_shape=(
            jax.ShapeDtypeStruct((TABLE_BLOCKS,) + block, BF16),
            jax.ShapeDtypeStruct((2, TILE), jnp.int32),
        ),
        in_specs=[vmem, vmem, smem, vmem, vmem, vmem],
        out_specs=(pl.BlockSpec(memory_space=pl.ANY), vmem),
        scratch_shapes=[
            pltpu.VMEM((OWN_BLOCKS,) + block, BF16),
            pltpu.VMEM((FAR_BLOCKS,) + block, BF16),
            pltpu.VMEM((HALO_RUN,) + block, BF16),
            pltpu.SemaphoreType.DMA((4, len(RUNS))),
            pltpu.SemaphoreType.DMA((4, len(RUNS))),
            pltpu.SemaphoreType.DMA,
            pltpu.SemaphoreType.DMA((4, len(RUNS))),
        ],
        compiler_params=pltpu.CompilerParams(
            collective_id=0, has_side_effects=True, vmem_limit_bytes=VMEM_LIMIT
        ),
        cost_estimate=pl.CostEstimate(
            flops=5 * 10**9, bytes_accessed=8 * 2**20, transcendentals=0
        ),
    )(nodes, send_rows, counts, halo_rows, send_idx, recv_idx)


def edge_kernel(
    meta_ref, edge_ref, cot_ref, snd_ref, rcv_ref, tab_ref, cota_ref,
    w1_ref, w2_ref, gain_ref,
    new_ref, grad_ref, agg_ref, far_ref, own_ref, pay_ref,
    ps_t, pr_t, ca_t, s_acc, ra_acc, fe_acc, w2_acc, g_acc, gain_b, w1_t, w2_t, fsr_acc,
):
    step = pl.program_id(0)
    steps = pl.num_programs(0)

    @pl.when(step == 0)
    def _prologue():
        for part in range(3):
            w1_t[part] = w1_ref[part * TILE : (part + 1) * TILE, :].T
        w2_t[...] = w2_ref[...].T
        gain_b[...] = jnp.broadcast_to(gain_ref[...], (TILE, TILE)).T

        def zero(b, _):
            s_acc[b] = jnp.zeros((TILE, TILE), F32)
            return 0

        lax.fori_loop(0, TABLE_BLOCKS, zero, 0, unroll=2)

        def zero_two(b, _):
            ra_acc[b] = jnp.zeros((TILE, 2 * TILE), F32)
            return 0

        lax.fori_loop(0, OWNED_BLOCKS, zero_two, 0, unroll=2)
        fe_acc[...] = jnp.zeros_like(fe_acc)
        w2_acc[...] = jnp.zeros_like(w2_acc)
        g_acc[...] = jnp.zeros_like(g_acc)

        def project(b, _):
            ps_t[b] = mm(w1_t[1], tab_ref[b]).astype(BF16)
            return 0

        lax.fori_loop(0, TABLE_BLOCKS, project, 0, unroll=4)

        def project_owned(b, _):
            pr_t[b] = mm(w1_t[2], tab_ref[b]).astype(BF16)
            ca_t[b] = cota_ref[pl.ds(pl.multiple_of(b * TILE, TILE), TILE), :].T
            return 0

        lax.fori_loop(0, OWNED_BLOCKS, project_owned, 0, unroll=4)

    we = w1_ref[:TILE, :]
    we_t = w1_t[0]
    w2 = w2_ref[...]
    gain = gain_b[...]
    gain2 = jnp.concatenate([gain, gain], axis=1)

    def pair(p, _):
        tile = (step * PAIRS + p) * 2
        first = pl.multiple_of(p * 2 * TILE, 2 * TILE)
        edges = edge_ref[pl.ds(first, 2 * TILE), :]
        edges_t = edges.T
        cot_t = cot_ref[pl.ds(first, 2 * TILE), :].T.astype(F32)
        hot_s, hot_r, near, cots, blocks = [], [], [], [], []
        for side in range(2):
            bs = meta_ref[0, tile + side]
            br = meta_ref[1, tile + side]
            blocks.append((bs, br))
            hs = onehot(TILE, snd_ref[pl.ds(tile + side, 1), :] & (TILE - 1), 0)
            hr = onehot(TILE, rcv_ref[pl.ds(tile + side, 1), :] & (TILE - 1), 0)
            hot_s.append(hs)
            hot_r.append(hr)
            near.append(
                mm(
                    jnp.concatenate([ps_t[bs], pr_t[br]], axis=1),
                    jnp.concatenate([hs, hr], axis=0),
                )
            )
            cots.append(mm(ca_t[br], hr))
        preact = mm(we_t, edges_t) + jnp.concatenate(near, axis=1)
        sig = 0.5 * jnp.tanh(0.5 * preact) + 0.5
        hidden = preact * sig
        slope = sig + hidden * (1.0 - sig)
        hidden = hidden.astype(BF16)
        output = mm(w2_t[...], hidden)
        centred = output - jnp.sum(output, axis=0, keepdims=True) * (1.0 / TILE)
        variance = jnp.sum(centred * centred, axis=0, keepdims=True) * (1.0 / TILE)
        inverse = lax.rsqrt(variance + EPS)
        normed = centred * inverse
        message = normed * gain2
        new_edge = (edges_t.astype(F32) + message).astype(BF16)
        new_ref[pl.ds(first, 2 * TILE), :] = new_edge.T
        message = message.astype(BF16)
        d_message = cot_t + jnp.concatenate(cots, axis=1)
        weighted = d_message * normed
        g_acc[...] += weighted
        d_norm = d_message * gain2
        mean_one = jnp.sum(d_norm, axis=0, keepdims=True) * (1.0 / TILE)
        mean_two = jnp.sum(weighted * gain2, axis=0, keepdims=True) * (1.0 / TILE)
        d_output = (inverse * (d_norm - mean_one - normed * mean_two)).astype(BF16)
        w2_acc[...] += mmt(hidden, d_output)
        d_preact = (mm(w2, d_output) * slope).astype(BF16)
        fe_acc[...] += mm(d_preact, edges)
        grad_edge = (cot_t + mm(we, d_preact)).astype(BF16)
        grad_ref[pl.ds(first, 2 * TILE), :] = grad_edge.T
        for side in range(2):
            bs, br = blocks[side]
            lanes = slice(side * TILE, (side + 1) * TILE)
            d_pre = d_preact[:, lanes]
            s_acc[bs] += mmt(hot_s[side], d_pre)
            both = jnp.concatenate([d_pre, message[:, lanes]], axis=0)
            ra_acc[br] += mmt(hot_r[side], both)
        return 0

    lax.fori_loop(0, PAIRS, pair, 0, unroll=2)

    @pl.when(step == steps - 1)
    def _epilogue():
        ws = w1_ref[TILE : 2 * TILE, :]
        wr = w1_ref[2 * TILE :, :]
        wsr = jnp.concatenate([ws, wr], axis=1)

        fsr_acc[...] = jnp.zeros_like(fsr_acc)

        def own(b, _):
            s = s_acc[b].astype(BF16)
            ra = ra_acc[b]
            r = ra[:, :TILE].astype(BF16)
            rows = pl.ds(pl.multiple_of(b * TILE, TILE), TILE)
            agg_ref[rows, :] = ra[:, TILE:].astype(BF16)
            both = jnp.concatenate([s, r], axis=1)
            own_ref[rows, :] = mmt(both, wsr)
            fsr_acc[...] += mm(tab_ref[b], both)
            return 0

        lax.fori_loop(0, OWN_BLOCKS, own, 0, unroll=4)

        def migrated(b, _):
            s = s_acc[b].astype(BF16)
            ra = ra_acc[b]
            r = ra[:, :TILE].astype(BF16)
            rows = pl.ds(pl.multiple_of(b * TILE, TILE), TILE)
            agg_ref[rows, :] = ra[:, TILE:].astype(BF16)
            both = jnp.concatenate([s, r], axis=1)
            far_ref[b - OWN_BLOCKS] = mmt(wsr, both).astype(BF16)
            fsr_acc[...] += mm(tab_ref[b], both)
            return 0

        lax.fori_loop(OWN_BLOCKS, OWNED_BLOCKS, migrated, 0, unroll=4)

        def halo(b, _):
            s = s_acc[b].astype(BF16)
            far_ref[b - OWN_BLOCKS] = mmt(ws, s).astype(BF16)
            fsr_acc[:, :TILE] += mm(tab_ref[b], s)
            return 0

        lax.fori_loop(OWNED_BLOCKS, TABLE_BLOCKS, halo, 0, unroll=4)
        first = fsr_acc[:, :TILE]
        second = fsr_acc[:, TILE:]
        edge_part = fe_acc[...].T
        w2_part = w2_acc[...]
        g_part = g_acc[:, :TILE] + g_acc[:, TILE:]
        g_row = jnp.sum(g_part.T, axis=0, keepdims=True)
        g_tile = jnp.broadcast_to(g_row, (CHUNK - WEIGHT_CHUNK, TILE))
        per = TILE // WEIGHT_CHUNK
        for n, part in enumerate((edge_part, first, second, w2_part)):
            for c in range(per):
                pay_ref[n * per + c, :WEIGHT_CHUNK, :] = part[
                    c * WEIGHT_CHUNK : (c + 1) * WEIGHT_CHUNK
                ]
                pay_ref[n * per + c, WEIGHT_CHUNK:, :] = g_tile


def edge_pass(meta, edges, cot_edge, send_idx, recv_idx, table, cot_agg, w_first, w_second, gain):
    rows = PAIRS * 2 * TILE
    steps = edges.shape[0] // rows
    block = (TILE, TILE)

    def whole(*shape):
        return pl.BlockSpec(shape, lambda s, m: (0,) * len(shape))

    stream = pl.BlockSpec((rows, TILE), lambda s, m: (s, 0))
    return pl.pallas_call(
        edge_kernel,
        name="edge_block",
        grid_spec=pltpu.PrefetchScalarGridSpec(
            num_scalar_prefetch=1,
            grid=(steps,),
            in_specs=[
                stream,
                stream,
                whole(*send_idx.shape),
                whole(*recv_idx.shape),
                whole(*table.shape),
                whole(*cot_agg.shape),
                whole(*w_first.shape),
                whole(*w_second.shape),
                whole(*gain.shape),
            ],
            out_specs=[
                stream,
                stream,
                whole(OWNED_BLOCKS * TILE, TILE),
                whole(FAR_BLOCKS, TILE, TILE),
                whole(OWN_BLOCKS * TILE, TILE),
                whole(RANKS, CHUNK, TILE),
            ],
            scratch_shapes=[
                pltpu.VMEM((TABLE_BLOCKS,) + block, BF16),
                pltpu.VMEM((OWNED_BLOCKS,) + block, BF16),
                pltpu.VMEM((OWNED_BLOCKS,) + block, BF16),
                pltpu.VMEM((TABLE_BLOCKS,) + block, F32),
                pltpu.VMEM((OWNED_BLOCKS, TILE, 2 * TILE), F32),
                pltpu.VMEM(block, F32),
                pltpu.VMEM(block, F32),
                pltpu.VMEM((TILE, 2 * TILE), F32),
                pltpu.VMEM(block, F32),
                pltpu.VMEM((3,) + block, BF16),
                pltpu.VMEM(block, BF16),
                pltpu.VMEM((TILE, 2 * TILE), F32),
            ],
        ),
        out_shape=[
            jax.ShapeDtypeStruct(edges.shape, BF16),
            jax.ShapeDtypeStruct(edges.shape, BF16),
            jax.ShapeDtypeStruct((OWNED_BLOCKS * TILE, TILE), BF16),
            jax.ShapeDtypeStruct((FAR_BLOCKS, TILE, TILE), BF16),
            jax.ShapeDtypeStruct((OWN_BLOCKS * TILE, TILE), F32),
            jax.ShapeDtypeStruct((RANKS, CHUNK, TILE), F32),
        ],
        compiler_params=pltpu.CompilerParams(vmem_limit_bytes=VMEM_LIMIT),
        cost_estimate=pl.CostEstimate(
            flops=12 * 10**9, bytes_accessed=24 * 2**20, transcendentals=3 * 2**20
        ),
    )(meta, edges, cot_edge, send_idx, recv_idx, table, cot_agg, w_first, w_second, gain)


def rank_device(rank):
    i = lax.axis_index("gx")
    j = lax.axis_index("gy")
    gx = (rank // 8) * 4 + (lax.rem(i, 4) // 2) * 2 + lax.rem(rank, 2)
    gy = lax.rem(rank // 2, 4) * 2 + lax.rem(j, 2)
    return gx, gy


def my_rank():
    i = lax.axis_index("gx")
    j = lax.axis_index("gy")
    return (i // 4) * 8 + (j // 2) * 2 + lax.rem(i, 2)


def column_device(place):
    i = lax.axis_index("gx")
    j = lax.axis_index("gy")
    return (i // 4) * 4 + (place // 2) * 2 + lax.rem(i, 2), (j // 2) * 2 + lax.rem(place, 2)


def my_place():
    i = lax.axis_index("gx")
    j = lax.axis_index("gy")
    return (lax.rem(i, 4) // 2) * 2 + lax.rem(j, 2)


def return_kernel(
    far_ref, own_ref, pay_ref, send_ref, count_ref, halo_ref,
    lat_ref, sum_ref,
    back, mine, ring, col, acc, got,
    send_sem, recv_sem, rs_send, rs_recv, col_send, col_recv, ag_send, ag_recv,
):
    rank = my_rank()
    place = my_place()
    barrier = pltpu.get_barrier_semaphore()
    greet_neighbours(barrier)

    def greet(s, _):
        device = rank_device(lax.rem(rank + s, RANKS))
        pl.semaphore_signal(barrier, inc=1, device_id=device, device_id_type=MESH)
        return 0

    lax.fori_loop(1, RANKS, greet, 0)
    for s in range(1, 4):
        device = column_device(lax.rem(place + s, 4))
        pl.semaphore_signal(barrier, inc=1, device_id=device, device_id_type=MESH)

    acc[:, :TILE] = own_ref[:HALF, :]
    acc[:, TILE:] = own_ref[HALF:, :]
    pl.semaphore_wait(barrier, neighbour_count() + RANKS - 1 + 3)

    def give(k, run, to_slot):
        return far_copy(far_ref, back, send_sem, recv_sem, k, run, 0, to_slot)

    for run in range(len(RUNS)):
        for k in (2, 3, 0, 1):
            copy, exists = give(k, run, k ^ 1)
            guarded(exists, copy.start)

    def scatter_copy(s):
        to = lax.rem(rank + s, RANKS)
        return pltpu.make_async_remote_copy(
            src_ref=pay_ref.at[to],
            dst_ref=ring.at[rank],
            send_sem=rs_send.at[s],
            recv_sem=rs_recv.at[s],
            device_id=rank_device(to),
            device_id_type=MESH,
        )

    def start_scatter(s, _):
        scatter_copy(s).start()
        return 0

    lax.fori_loop(1, RANKS, start_scatter, 0)

    def wait_scatter(s, _):
        scatter_copy(s).wait()
        return 0

    lax.fori_loop(1, RANKS, wait_scatter, 0)

    ring[rank] = pay_ref[rank]

    def add_up(s, total):
        return total + ring[s]

    col[0] = lax.fori_loop(1, RANKS, add_up, ring[0], unroll=8)

    def column_copy(s):
        return pltpu.make_async_remote_copy(
            src_ref=col.at[0],
            dst_ref=col.at[s],
            send_sem=col_send.at[s],
            recv_sem=col_recv.at[s],
            device_id=column_device(lax.rem(place + s, 4)),
            device_id_type=MESH,
        )

    for s in range(1, 4):
        column_copy(s).start()

    slot = lax.broadcasted_iota(jnp.int32, (1, TILE), 1)

    def spread(index, values_t):
        upper = jnp.broadcast_to(index >= HALF, values_t.shape)
        none = jnp.zeros((), BF16)
        right = jnp.concatenate(
            [jnp.where(upper, none, values_t), jnp.where(upper, values_t, none)], axis=0
        )
        low = jnp.where(index >= HALF, index - HALF, index)

        def piece(m, _):
            first = pl.multiple_of(m * 2 * TILE, 2 * TILE)
            hot = onehot(2 * TILE, low, first)
            acc[pl.ds(first, 2 * TILE), :] += mmt(hot, right)
            return 0

        lax.fori_loop(0, HALF // (2 * TILE), piece, 0)

    for k in range(4):
        copy, exists = give(k, 0, k)
        guarded(exists, copy.wait_recv)
        copy, exists = give(k, 0, k ^ 1)
        guarded(exists, copy.wait_send)
    indices, values = [], []
    for k in range(4):
        _, exists = neighbour(k)
        live = slot < count_ref[k]
        if exists is not None:
            live = jnp.logical_and(live, exists)
        indices.append(jnp.where(live, send_ref[pl.ds(k, 1), :], -1))
        blockv = back[k]
        if exists is not None:
            blockv = jnp.where(jnp.broadcast_to(live, (TILE, TILE)), blockv, jnp.zeros((), BF16))
        values.append(blockv)
    spread(jnp.concatenate(indices, axis=1), jnp.concatenate(values, axis=1))

    for s in range(1, 4):
        column_copy(s).wait()
    total = (col[0] + col[2]) + (col[1] + col[3])
    mine[...] = total[:WEIGHT_CHUNK]
    got[rank] = total[:WEIGHT_CHUNK]
    sum_ref[pl.ds(RANKS * WEIGHT_CHUNK, CHUNK - WEIGHT_CHUNK), :] = total[WEIGHT_CHUNK:]

    def gather_copy(s, owner):
        return pltpu.make_async_remote_copy(
            src_ref=mine,
            dst_ref=got.at[owner],
            send_sem=ag_send.at[s],
            recv_sem=ag_recv.at[s],
            device_id=rank_device(lax.rem(rank + s, RANKS)),
            device_id_type=MESH,
        )

    def start_gather(s, _):
        gather_copy(s, rank).start()
        return 0

    lax.fori_loop(1, RANKS, start_gather, 0)

    for run in range(1, len(RUNS)):
        at, count = RUNS[run]
        for k in (0, 1, 2, 3):
            copy, exists = give(k, run, k)

            def take(copy=copy, k=k, at=at, count=count):
                copy.wait_recv()
                first = table_place(k, at)
                index = halo_ref[pl.ds(k, 1), pl.ds((at - 1) * TILE, count * TILE)]
                spread(index, jnp.concatenate([back[first + n] for n in range(count)], axis=1))

            guarded(exists, take)
    for run in range(1, len(RUNS)):
        for k in range(4):
            copy, exists = give(k, run, k ^ 1)
            guarded(exists, copy.wait_send)

    def wait_gather(s, _):
        owner = lax.rem(rank + RANKS - s, RANKS)
        gather_copy(s, owner).wait()
        return 0

    lax.fori_loop(1, RANKS, wait_gather, 0)
    for c in range(RANKS):
        sum_ref[c * WEIGHT_CHUNK : (c + 1) * WEIGHT_CHUNK, :] = got[c]
    lat_ref[:HALF, :] = acc[:, :TILE]
    lat_ref[HALF:, :] = acc[:, TILE:]


def give_back(far, own, payload, send_rows, counts, halo_rows):
    vmem = pl.BlockSpec(memory_space=pltpu.VMEM)
    smem = pl.BlockSpec(memory_space=pltpu.SMEM)
    dma = pltpu.SemaphoreType.DMA
    return pl.pallas_call(
        return_kernel,
        name="return_rows",
        out_shape=(
            jax.ShapeDtypeStruct((OWN_BLOCKS * TILE, TILE), F32),
            jax.ShapeDtypeStruct((RANKS * WEIGHT_CHUNK + CHUNK - WEIGHT_CHUNK, TILE), F32),
        ),
        in_specs=[vmem, vmem, vmem, vmem, smem, vmem],
        out_specs=(vmem, vmem),
        scratch_shapes=[
            pltpu.VMEM((FAR_BLOCKS, TILE, TILE), BF16),
            pltpu.VMEM((WEIGHT_CHUNK, TILE), F32),
            pltpu.VMEM((RANKS, CHUNK, TILE), F32),
            pltpu.VMEM((4, CHUNK, TILE), F32),
            pltpu.VMEM((HALF, 2 * TILE), F32),
            pltpu.VMEM((RANKS, WEIGHT_CHUNK, TILE), F32),
            dma((4, len(RUNS))),
            dma((4, len(RUNS))),
            dma((RANKS,)),
            dma((RANKS,)),
            dma((4,)),
            dma((4,)),
            dma((RANKS,)),
            dma((RANKS,)),
        ],
        compiler_params=pltpu.CompilerParams(
            collective_id=1, has_side_effects=True, vmem_limit_bytes=VMEM_LIMIT
        ),
        cost_estimate=pl.CostEstimate(
            flops=5 * 10**9, bytes_accessed=8 * 2**20, transcendentals=0
        ),
    )(far, own, payload, send_rows, counts, halo_rows)


def per_device(
    latent,
    edge_state,
    w_first,
    w_second,
    norm_gain,
    send_list,
    send_count,
    halo_list,
    senders,
    receivers,
    cotangent_edge,
    cotangent_agg,
):
    send_rows = send_list[0, 0]
    halo_rows = halo_list[0, 0]
    counts = send_count[0, 0]
    send_idx = senders.reshape(-1, TILE)
    recv_idx = receivers.reshape(-1, TILE)
    table, meta = fetch(latent[0, 0], send_rows, counts, halo_rows, send_idx, recv_idx)
    new_edge, grad_edge, aggregate, far, own, payload = edge_pass(
        meta,
        edge_state[0, 0],
        cotangent_edge[0, 0],
        send_idx,
        recv_idx,
        table,
        cotangent_agg[0, 0],
        w_first,
        w_second,
        norm_gain.reshape(1, TILE),
    )
    grad_latent, sums = give_back(far, own, payload, send_rows, counts, halo_rows)
    return (
        new_edge[None, None],
        aggregate[None, None],
        grad_edge[None, None],
        grad_latent[None, None],
        sums[: 3 * TILE],
        sums[3 * TILE : 4 * TILE],
        sums[4 * TILE],
    )


def solution(mesh):
    rows = P("gx", "gy", None, None)
    flat = P("gx", "gy", None)
    in_specs = (rows, rows, P(), P(), P(), rows, flat, rows, flat, flat, rows, rows)
    out_specs = (rows, rows, rows, rows, P(), P(), P())
    return jax.shard_map(
        per_device, mesh=mesh, in_specs=in_specs, out_specs=out_specs, check_vma=False
    )
```

time: 408 us -> 155 us (0.38); the launches traced: 401 us -> 152 us
  Pallas kernels: 0 us -> 144 us
  matrix products: 104 us -> 0 us
  other arithmetic: 72.8 us -> 0 us
  blocking collectives: 67.8 us -> 0 us
  local copies, waits for them, and re-layouts: 61.5 us -> 7.32 us
  starting transfers between devices: 40.8 us -> 0 us
  waiting for transfers between devices: 39.1 us -> 0 us
  between operations: 14.9 us -> 0.65 us
    pallas_call x0 -> x3, Pallas kernels: none -> 144 us  [the longest x1 68.4 us: edge_pass(): pl.pallas_call(edge_kernel, name='edge_block', grid_spec=pltpu.PrefetchSc...]
    dot_general x24 -> x0, matrix products: 104 us -> none  [the longest x3 29.8 us: spread_rows(): jnp.dot(choose.T, per_tile.reshape(tiles, tile_rows * width), precision=l...]
    psum x1 -> x0, blocking collectives: 67.8 us -> none  [per_device(): lax.psum((d_first, d_second, d_gain), ('gx', 'gy'))]
    ppermute x16 -> x0, starting transfers between devices: 40.8 us -> none  [the longest x8 28.7 us: extended(): lax.ppermute(tail, axis, [(i, (i + 1) % count) for i in range(ends)])]
    psum x1 -> x0, waiting for transfers between devices: 36.4 us -> none  [per_device(): lax.psum((d_first, d_second, d_gain), ('gx', 'gy'))]
    scatter-add x2 -> x0, other arithmetic: 27.5 us -> none  [the longest x1 23.4 us: per_device(): grad_latent.at[halo_rows.reshape(-1)].add(back_halo.reshape(-1, width))]
    unnamed x73 -> x1, local copies, waits for them, and re-layouts: 19 us -> 3.04 us
    broadcast_in_dim x1 -> x0, other arithmetic: 15.6 us -> none  [per_device(): new_edge[None, None]]
  transfers between devices with their start and end apart: 17 -> 0, of which waited for: 3 -> 0; matrix products, arithmetic and copies ran while one was open for 24% -> 0% of each run, Pallas kernels for 0% -> 0%
where the time goes in v1:
time: 155 us; the launch traced here: 152 us
  Pallas kernels  144 us (93%)
  local copies, waits for them, and re-layouts  7.32 us (5%)
    pallas_call x1, Pallas kernels, edge_pass(): pl.pallas_call(edge_kernel, name='edge_block', grid_spec=pltpu.PrefetchSc...  68.4 us
    pallas_call x1, Pallas kernels, give_back(): pl.pallas_call(return_kernel, name='return_rows', out_shape=(jax.ShapeDty...  47.6 us
    pallas_call x1, Pallas kernels, fetch(): pl.pallas_call(fetch_kernel, name='fetch_rows', out_shape=(jax.ShapeDtype...  28 us

profile of v1, /device:TPU:1, one launch (start us, length us, event | category | flops | bytes accessed | tf_op | source)
XLA Modules:
  0.0 152.0 jit_solution(5060594915463221302)
XLA Ops:
  0.6 28.0 %fetch_rows.1 = (bf16[68,128,128]{2,1,0:T(8,128)(2,1)}, s32[2,128]{1,0:T(2,128)}) custom-call(bf16[4096,128]{1,0:T(8,128)(2,1)} %bitcast.20, s32[4,128]{1,0:T(4,128)} %bitcast.27, s32[4]{0:T(128)} %bitcast.30, s32[4,1024]{1,0:T(4,128)} %bitcast.25, s32[128,128]{1,0:T(8,128)} %bitcast.21, s32[128,128]{1,0:T(8,128)} %bitcast.23), custom_call_target="tpu_custom_call" | custom-call | flops 5000000000 | bytes 8388608 | tf_op jit(solution)/shard_map/fetch_rows/pallas_call | solution.py:222
  28.7 68.4 %edge_block.1 = (bf16[16384,128]{1,0:T(8,128)(2,1)}, bf16[16384,128]{1,0:T(8,128)(2,1)}, bf16[4608,128]{1,0:T(8,128)(2,1)}, bf16[36,128,128]{2,1,0:T(8,128)(2,1)...) custom-call(s32[2,128]{1,0:T(2,128)} %get-tuple-element.17.meta_ref, bf16[16384,128]{1,0:T(8,128)(2,1)} %bitcast.17, ...), custom_call_target="tpu_custom_call" | custom-call | flops 12000000000 | bytes 25165824 | tf_op jit(solution)/shard_map/edge_block/pallas_call | solution.py:424
  97.1 47.6 %return_rows.1 = (f32[4096,128]{1,0:T(8,128)}, f32[520,128]{1,0:T(8,128)}) custom-call(bf16[36,128,128]{2,1,0:T(8,128)(2,1)} %get-tuple-element.22.far_ref, f32[4096,128]{1,0:T(8,128)} %get-tuple-element.23.own_ref, f32[32,24,128]{2,1,0:T(8,128)} %get-tuple-element.24.pay_ref, s32[4,128]{1,0:T(4,128)} %bitcast.28, s32[4]{0:T(128)} %bitcast.31, ...), custom_call_target="tpu_custom_call" | custom-call | flops 5000000000 | bytes 8388608 | tf_op jit(solution)/shard_map/return_rows/pallas_call | solution.py:673
  144.7 1.2 slice_bitcast_fusion
  145.9 1.5 slice.10
  147.4 1.6 %slice.9 = f32[384,128]{1,0:T(8,128)} slice(f32[520,128]{1,0:T(8,128)} %get-tuple-element.26), slice={[0:384], [0:128]} | slice | bytes 393216 | tf_op jit(solution)/shard_map/slice | solution.py:745
  149.0 3.0 %copy.20 = f32[1,1,4096,128]{3,2,1,0:T(8,128)} copy(f32[1,1,4096,128]{3,2,1,0:T(8,128)} %bitcast.16) | data formatting | bytes 4194304

commit v2 on v1

--- a/solution.py
+++ b/solution.py
@@ -22,10 +22,13 @@
 TABLE_BLOCKS = OWN_BLOCKS + FAR_BLOCKS
 PER_DIR = HALO_BLOCKS // 4
 HALF = OWN_BLOCKS * TILE // 2
-PAIRS = 4
+GROUP = 16
+GROUPS = 1
+UNROLL = 1
 RANKS = 32
 CHUNK = 24
 VMEM_LIMIT = 62 * 2**20
+RETURN_LIMIT = 24 * 2**20
 WEIGHT_CHUNK = 16
 
 
@@ -78,8 +81,17 @@
     return 2 + jnp.where(j > 0, 1, 0) + jnp.where(j < N_GY - 1, 1, 0)
 
 
-HALO_RUN = 4
-RUNS = [(0, 1)] + [(1 + at, HALO_RUN) for at in range(0, PER_DIR, HALO_RUN)]
+X_RUNS = ((0, 1), (1, 4), (5, 4))
+Y_RUNS = ((0, 1), (1, 4), (5, 2), (7, 2))
+RUNS = (X_RUNS, X_RUNS, Y_RUNS, Y_RUNS)
+MOST_RUNS = 4
+LONGEST = 4
+ORDER = (
+    [(k, 0) for k in (2, 3, 0, 1)]
+    + [(k, run) for run in (1, 2) for k in (0, 1)]
+    + [(k, run) for run in (1, 2, 3) for k in (2, 3)]
+)
+X_END = 4 + 4
 
 
 def table_place(direction, at):
@@ -89,7 +101,7 @@
 
 
 def far_copy(src, dst, send_sem, recv_sem, k, run, base, to_slot):
-    at, count = RUNS[run]
+    at, count = RUNS[k][run]
     device, exists = neighbour(k)
     copy = pltpu.make_async_remote_copy(
         src_ref=src.at[pl.ds(table_place(k, at), count)],
@@ -128,7 +140,7 @@
                 tab_ref.at[pl.ds(OWN_BLOCKS + table_place(k, at), count)],
                 zero_sem.at[k, run],
             )
-            for run, (at, count) in enumerate(RUNS)
+            for run, (at, count) in enumerate(RUNS[k])
         ]
 
     for k in (2, 3):
@@ -174,11 +186,9 @@
         copy, exists = far_copy(out_buf, tab_ref, send_sem, recv_sem, k, run, OWN_BLOCKS, k ^ 1)
         guarded(exists, copy.start)
 
-    for k in (2, 3, 0, 1):
-        start(k, 0)
-    for run in range(1, len(RUNS)):
-        at, count = RUNS[run]
-        for k in (2, 3, 0, 1):
+    for k, run in ORDER:
+        at, count = RUNS[k][run]
+        if at:
 
             def gather(step, _, k=k, at=at):
                 first = pl.multiple_of((at - 1) * TILE + step * 2 * TILE, 2 * TILE)
@@ -189,7 +199,7 @@
                 return 0
 
             lax.fori_loop(0, count // 2, gather, 0)
-            start(k, run)
+        start(k, run)
 
     firsts = lax.shift_right_logical(
         jnp.concatenate([snd_ref[...].T[:1], rcv_ref[...].T[:1]], axis=0), 7
@@ -205,14 +215,11 @@
                 copy.wait()
 
         pl.when(jnp.logical_not(exists))(drain)
-    for run in range(len(RUNS)):
-        for k in range(4):
-            copy, exists = far_copy(
-                out_buf, tab_ref, send_sem, recv_sem, k, run, OWN_BLOCKS, k ^ 1
-            )
-            guarded(exists, copy.wait_send)
-            back, exists = far_copy(out_buf, tab_ref, send_sem, recv_sem, k, run, OWN_BLOCKS, k)
-            guarded(exists, back.wait_recv)
+    for k, run in ORDER:
+        copy, exists = far_copy(out_buf, tab_ref, send_sem, recv_sem, k, run, OWN_BLOCKS, k ^ 1)
+        guarded(exists, copy.wait_send)
+        back, exists = far_copy(out_buf, tab_ref, send_sem, recv_sem, k, run, OWN_BLOCKS, k)
+        guarded(exists, back.wait_recv)
 
 
 def fetch(nodes, send_rows, counts, halo_rows, send_idx, recv_idx):
@@ -231,11 +238,11 @@
         scratch_shapes=[
             pltpu.VMEM((OWN_BLOCKS,) + block, BF16),
             pltpu.VMEM((FAR_BLOCKS,) + block, BF16),
-            pltpu.VMEM((HALO_RUN,) + block, BF16),
-            pltpu.SemaphoreType.DMA((4, len(RUNS))),
-            pltpu.SemaphoreType.DMA((4, len(RUNS))),
+            pltpu.VMEM((LONGEST,) + block, BF16),
+            pltpu.SemaphoreType.DMA((4, MOST_RUNS)),
+            pltpu.SemaphoreType.DMA((4, MOST_RUNS)),
             pltpu.SemaphoreType.DMA,
-            pltpu.SemaphoreType.DMA((4, len(RUNS))),
+            pltpu.SemaphoreType.DMA((4, MOST_RUNS)),
         ],
         compiler_params=pltpu.CompilerParams(
             collective_id=0, has_side_effects=True, vmem_limit_bytes=VMEM_LIMIT
@@ -277,33 +284,44 @@
         w2_acc[...] = jnp.zeros_like(w2_acc)
         g_acc[...] = jnp.zeros_like(g_acc)
 
-        def project(b, _):
-            ps_t[b] = mm(w1_t[1], tab_ref[b]).astype(BF16)
+        def project(at, _):
+            first = at * 4
+            blocks = jnp.concatenate([tab_ref[first + n] for n in range(4)], axis=1)
+            out = mm(w1_t[1], blocks).astype(BF16)
+            for n in range(4):
+                ps_t[first + n] = out[:, n * TILE : (n + 1) * TILE]
             return 0
 
-        lax.fori_loop(0, TABLE_BLOCKS, project, 0, unroll=4)
-
-        def project_owned(b, _):
-            pr_t[b] = mm(w1_t[2], tab_ref[b]).astype(BF16)
-            ca_t[b] = cota_ref[pl.ds(pl.multiple_of(b * TILE, TILE), TILE), :].T
+        lax.fori_loop(0, TABLE_BLOCKS // 4, project, 0)
+
+        def project_owned(at, _):
+            first = at * 4
+            blocks = jnp.concatenate([tab_ref[first + n] for n in range(4)], axis=1)
+            out = mm(w1_t[2], blocks).astype(BF16)
+            rows = pl.ds(pl.multiple_of(first * TILE, 4 * TILE), 4 * TILE)
+            turned = cota_ref[rows, :].T
+            for n in range(4):
+                pr_t[first + n] = out[:, n * TILE : (n + 1) * TILE]
+                ca_t[first + n] = turned[:, n * TILE : (n + 1) * TILE]
             return 0
 
-        lax.fori_loop(0, OWNED_BLOCKS, project_owned, 0, unroll=4)
+        lax.fori_loop(0, OWNED_BLOCKS // 4, project_owned, 0)
 
     we = w1_ref[:TILE, :]
     we_t = w1_t[0]
     w2 = w2_ref[...]
-    gain = gain_b[...]
-    gain2 = jnp.concatenate([gain, gain], axis=1)
-
-    def pair(p, _):
-        tile = (step * PAIRS + p) * 2
-        first = pl.multiple_of(p * 2 * TILE, 2 * TILE)
-        edges = edge_ref[pl.ds(first, 2 * TILE), :]
+    gain = jnp.concatenate([gain_b[...]] * GROUP, axis=1)
+    wide = GROUP * TILE
+
+    def group(p, _):
+        tile = (step * GROUPS + p) * GROUP
+        first = pl.multiple_of(p * wide, wide)
+        rows = pl.ds(first, wide)
+        edges = edge_ref[rows, :]
         edges_t = edges.T
-        cot_t = cot_ref[pl.ds(first, 2 * TILE), :].T.astype(F32)
+        cot_t = cot_ref[rows, :].T.astype(F32)
         hot_s, hot_r, near, cots, blocks = [], [], [], [], []
-        for side in range(2):
+        for side in range(GROUP):
             bs = meta_ref[0, tile + side]
             br = meta_ref[1, tile + side]
             blocks.append((bs, br))
@@ -328,23 +346,26 @@
         variance = jnp.sum(centred * centred, axis=0, keepdims=True) * (1.0 / TILE)
         inverse = lax.rsqrt(variance + EPS)
         normed = centred * inverse
-        message = normed * gain2
+        message = normed * gain
         new_edge = (edges_t.astype(F32) + message).astype(BF16)
-        new_ref[pl.ds(first, 2 * TILE), :] = new_edge.T
+        new_ref[rows, :] = new_edge.T
         message = message.astype(BF16)
         d_message = cot_t + jnp.concatenate(cots, axis=1)
         weighted = d_message * normed
-        g_acc[...] += weighted
-        d_norm = d_message * gain2
+        g_sum = weighted[:, :TILE]
+        for side in range(1, GROUP):
+            g_sum += weighted[:, side * TILE : (side + 1) * TILE]
+        g_acc[...] += g_sum
+        d_norm = d_message * gain
         mean_one = jnp.sum(d_norm, axis=0, keepdims=True) * (1.0 / TILE)
-        mean_two = jnp.sum(weighted * gain2, axis=0, keepdims=True) * (1.0 / TILE)
+        mean_two = jnp.sum(weighted * gain, axis=0, keepdims=True) * (1.0 / TILE)
         d_output = (inverse * (d_norm - mean_one - normed * mean_two)).astype(BF16)
         w2_acc[...] += mmt(hidden, d_output)
         d_preact = (mm(w2, d_output) * slope).astype(BF16)
         fe_acc[...] += mm(d_preact, edges)
         grad_edge = (cot_t + mm(we, d_preact)).astype(BF16)
-        grad_ref[pl.ds(first, 2 * TILE), :] = grad_edge.T
-        for side in range(2):
+        grad_ref[rows, :] = grad_edge.T
+        for side in range(GROUP):
             bs, br = blocks[side]
             lanes = slice(side * TILE, (side + 1) * TILE)
             d_pre = d_preact[:, lanes]
@@ -353,7 +374,7 @@
             ra_acc[br] += mmt(hot_r[side], both)
         return 0
 
-    lax.fori_loop(0, PAIRS, pair, 0, unroll=2)
+    lax.fori_loop(0, GROUPS, group, 0, unroll=UNROLL)
 
     @pl.when(step == steps - 1)
     def _epilogue():
@@ -363,45 +384,45 @@
 
         fsr_acc[...] = jnp.zeros_like(fsr_acc)
 
-        def own(b, _):
-            s = s_acc[b].astype(BF16)
-            ra = ra_acc[b]
-            r = ra[:, :TILE].astype(BF16)
-            rows = pl.ds(pl.multiple_of(b * TILE, TILE), TILE)
-            agg_ref[rows, :] = ra[:, TILE:].astype(BF16)
+        def owned(at):
+            first = at * 4
+            rows = pl.ds(pl.multiple_of(first * TILE, 4 * TILE), 4 * TILE)
+            s = jnp.concatenate([s_acc[first + n].astype(BF16) for n in range(4)], axis=0)
+            ra = [ra_acc[first + n] for n in range(4)]
+            r = jnp.concatenate([x[:, :TILE].astype(BF16) for x in ra], axis=0)
+            agg_ref[rows, :] = jnp.concatenate([x[:, TILE:].astype(BF16) for x in ra], axis=0)
             both = jnp.concatenate([s, r], axis=1)
+            tab = jnp.concatenate([tab_ref[first + n] for n in range(4)], axis=1)
+            fsr_acc[...] += mm(tab, both)
+            return rows, both
+
+        def own(at, _):
+            rows, both = owned(at)
             own_ref[rows, :] = mmt(both, wsr)
-            fsr_acc[...] += mm(tab_ref[b], both)
             return 0
 
-        lax.fori_loop(0, OWN_BLOCKS, own, 0, unroll=4)
-
-        def migrated(b, _):
-            s = s_acc[b].astype(BF16)
-            ra = ra_acc[b]
-            r = ra[:, :TILE].astype(BF16)
-            rows = pl.ds(pl.multiple_of(b * TILE, TILE), TILE)
-            agg_ref[rows, :] = ra[:, TILE:].astype(BF16)
-            both = jnp.concatenate([s, r], axis=1)
-            far_ref[b - OWN_BLOCKS] = mmt(wsr, both).astype(BF16)
-            fsr_acc[...] += mm(tab_ref[b], both)
+        lax.fori_loop(0, OWN_BLOCKS // 4, own, 0)
+        _, both = owned(OWN_BLOCKS // 4)
+        back = mmt(wsr, both).astype(BF16)
+        for n in range(MIG_BLOCKS):
+            far_ref[n] = back[:, n * TILE : (n + 1) * TILE]
+
+        def halo(at, _):
+            first = OWNED_BLOCKS + at * 4
+            s = jnp.concatenate([s_acc[first + n].astype(BF16) for n in range(4)], axis=0)
+            back = mmt(ws, s).astype(BF16)
+            for n in range(4):
+                far_ref[first - OWN_BLOCKS + n] = back[:, n * TILE : (n + 1) * TILE]
+            tab = jnp.concatenate([tab_ref[first + n] for n in range(4)], axis=1)
+            fsr_acc[:, :TILE] += mm(tab, s)
             return 0
 
-        lax.fori_loop(OWN_BLOCKS, OWNED_BLOCKS, migrated, 0, unroll=4)
-
-        def halo(b, _):
-            s = s_acc[b].astype(BF16)
-            far_ref[b - OWN_BLOCKS] = mmt(ws, s).astype(BF16)
-            fsr_acc[:, :TILE] += mm(tab_ref[b], s)
-            return 0
-
-        lax.fori_loop(OWNED_BLOCKS, TABLE_BLOCKS, halo, 0, unroll=4)
+        lax.fori_loop(0, HALO_BLOCKS // 4, halo, 0)
         first = fsr_acc[:, :TILE]
         second = fsr_acc[:, TILE:]
         edge_part = fe_acc[...].T
         w2_part = w2_acc[...]
-        g_part = g_acc[:, :TILE] + g_acc[:, TILE:]
-        g_row = jnp.sum(g_part.T, axis=0, keepdims=True)
+        g_row = jnp.sum(g_acc[...].T, axis=0, keepdims=True)
         g_tile = jnp.broadcast_to(g_row, (CHUNK - WEIGHT_CHUNK, TILE))
         per = TILE // WEIGHT_CHUNK
         for n, part in enumerate((edge_part, first, second, w2_part)):
@@ -413,7 +434,7 @@
 
 
 def edge_pass(meta, edges, cot_edge, send_idx, recv_idx, table, cot_agg, w_first, w_second, gain):
-    rows = PAIRS * 2 * TILE
+    rows = GROUPS * GROUP * TILE
     steps = edges.shape[0] // rows
     block = (TILE, TILE)
 
@@ -454,7 +475,7 @@
                 pltpu.VMEM((OWNED_BLOCKS, TILE, 2 * TILE), F32),
                 pltpu.VMEM(block, F32),
                 pltpu.VMEM(block, F32),
-                pltpu.VMEM((TILE, 2 * TILE), F32),
+                pltpu.VMEM(block, F32),
                 pltpu.VMEM(block, F32),
                 pltpu.VMEM((3,) + block, BF16),
                 pltpu.VMEM(block, BF16),
@@ -503,9 +524,9 @@
 
 
 def return_kernel(
-    far_ref, own_ref, pay_ref, send_ref, count_ref, halo_ref,
-    lat_ref, sum_ref,
-    back, mine, ring, col, acc, got,
+    far_ref, pay_ref, send_ref, count_ref, halo_ref,
+    acc, sum_ref,
+    back, mine, ring, col, got, pay_sem,
     send_sem, recv_sem, rs_send, rs_recv, col_send, col_recv, ag_send, ag_recv,
 ):
     rank = my_rank()
@@ -523,17 +544,13 @@
         device = column_device(lax.rem(place + s, 4))
         pl.semaphore_signal(barrier, inc=1, device_id=device, device_id_type=MESH)
 
-    acc[:, :TILE] = own_ref[:HALF, :]
-    acc[:, TILE:] = own_ref[HALF:, :]
+    pay_copy = pltpu.make_async_copy(pay_ref.at[rank], ring.at[rank], pay_sem)
+    pay_copy.start()
+    acc[...] = jnp.zeros_like(acc)
     pl.semaphore_wait(barrier, neighbour_count() + RANKS - 1 + 3)
 
     def give(k, run, to_slot):
         return far_copy(far_ref, back, send_sem, recv_sem, k, run, 0, to_slot)
-
-    for run in range(len(RUNS)):
-        for k in (2, 3, 0, 1):
-            copy, exists = give(k, run, k ^ 1)
-            guarded(exists, copy.start)
 
     def scatter_copy(s):
         to = lax.rem(rank + s, RANKS)
@@ -552,13 +569,20 @@
 
     lax.fori_loop(1, RANKS, start_scatter, 0)
 
+    def start_give(order):
+        for k, run in order:
+            copy, exists = give(k, run, k ^ 1)
+            guarded(exists, copy.start)
+
+    start_give(ORDER[:X_END])
+
     def wait_scatter(s, _):
         scatter_copy(s).wait()
         return 0
 
     lax.fori_loop(1, RANKS, wait_scatter, 0)
 
-    ring[rank] = pay_ref[rank]
+    pay_copy.wait()
 
     def add_up(s, total):
         return total + ring[s]
@@ -577,6 +601,7 @@
 
     for s in range(1, 4):
         column_copy(s).start()
+    start_give(ORDER[X_END:])
 
     slot = lax.broadcasted_iota(jnp.int32, (1, TILE), 1)
 
@@ -587,14 +612,15 @@
             [jnp.where(upper, none, values_t), jnp.where(upper, values_t, none)], axis=0
         )
         low = jnp.where(index >= HALF, index - HALF, index)
+        right = right.T
 
         def piece(m, _):
             first = pl.multiple_of(m * 2 * TILE, 2 * TILE)
             hot = onehot(2 * TILE, low, first)
-            acc[pl.ds(first, 2 * TILE), :] += mmt(hot, right)
+            acc[pl.ds(first, 2 * TILE), :] += mm(hot, right)
             return 0
 
-        lax.fori_loop(0, HALF // (2 * TILE), piece, 0)
+        lax.fori_loop(0, HALF // (2 * TILE), piece, 0, unroll=8)
 
     for k in range(4):
         copy, exists = give(k, 0, k)
@@ -614,6 +640,20 @@
         values.append(blockv)
     spread(jnp.concatenate(indices, axis=1), jnp.concatenate(values, axis=1))
 
+    def take_all(order):
+        for k, run in order:
+            at, count = RUNS[k][run]
+            copy, exists = give(k, run, k)
+
+            def take(copy=copy, k=k, at=at, count=count):
+                copy.wait_recv()
+                first = table_place(k, at)
+                index = halo_ref[pl.ds(k, 1), pl.ds((at - 1) * TILE, count * TILE)]
+                spread(index, jnp.concatenate([back[first + n] for n in range(count)], axis=1))
+
+            guarded(exists, take)
+
+    take_all(ORDER[4:X_END])
     for s in range(1, 4):
         column_copy(s).wait()
     total = (col[0] + col[2]) + (col[1] + col[3])
@@ -637,22 +677,10 @@
 
     lax.fori_loop(1, RANKS, start_gather, 0)
 
-    for run in range(1, len(RUNS)):
-        at, count = RUNS[run]
-        for k in (0, 1, 2, 3):
-            copy, exists = give(k, run, k)
-
-            def take(copy=copy, k=k, at=at, count=count):
-                copy.wait_recv()
-                first = table_place(k, at)
-                index = halo_ref[pl.ds(k, 1), pl.ds((at - 1) * TILE, count * TILE)]
-                spread(index, jnp.concatenate([back[first + n] for n in range(count)], axis=1))
-
-            guarded(exists, take)
-    for run in range(1, len(RUNS)):
-        for k in range(4):
-            copy, exists = give(k, run, k ^ 1)
-            guarded(exists, copy.wait_send)
+    take_all(ORDER[X_END:])
+    for k, run in ORDER[4:]:
+        copy, exists = give(k, run, k ^ 1)
+        guarded(exists, copy.wait_send)
 
     def wait_gather(s, _):
         owner = lax.rem(rank + RANKS - s, RANKS)
@@ -662,32 +690,31 @@
     lax.fori_loop(1, RANKS, wait_gather, 0)
     for c in range(RANKS):
         sum_ref[c * WEIGHT_CHUNK : (c + 1) * WEIGHT_CHUNK, :] = got[c]
-    lat_ref[:HALF, :] = acc[:, :TILE]
-    lat_ref[HALF:, :] = acc[:, TILE:]
-
-
-def give_back(far, own, payload, send_rows, counts, halo_rows):
+
+
+def give_back(far, payload, send_rows, counts, halo_rows):
     vmem = pl.BlockSpec(memory_space=pltpu.VMEM)
     smem = pl.BlockSpec(memory_space=pltpu.SMEM)
+    hbm = pl.BlockSpec(memory_space=pl.ANY)
     dma = pltpu.SemaphoreType.DMA
     return pl.pallas_call(
         return_kernel,
         name="return_rows",
         out_shape=(
-            jax.ShapeDtypeStruct((OWN_BLOCKS * TILE, TILE), F32),
+            jax.ShapeDtypeStruct((HALF, 2 * TILE), F32),
             jax.ShapeDtypeStruct((RANKS * WEIGHT_CHUNK + CHUNK - WEIGHT_CHUNK, TILE), F32),
         ),
-        in_specs=[vmem, vmem, vmem, vmem, smem, vmem],
+        in_specs=[hbm, hbm, vmem, smem, vmem],
         out_specs=(vmem, vmem),
         scratch_shapes=[
             pltpu.VMEM((FAR_BLOCKS, TILE, TILE), BF16),
             pltpu.VMEM((WEIGHT_CHUNK, TILE), F32),
             pltpu.VMEM((RANKS, CHUNK, TILE), F32),
             pltpu.VMEM((4, CHUNK, TILE), F32),
-            pltpu.VMEM((HALF, 2 * TILE), F32),
             pltpu.VMEM((RANKS, WEIGHT_CHUNK, TILE), F32),
-            dma((4, len(RUNS))),
-            dma((4, len(RUNS))),
+            dma,
+            dma((4, MOST_RUNS)),
+            dma((4, MOST_RUNS)),
             dma((RANKS,)),
             dma((RANKS,)),
             dma((4,)),
@@ -696,12 +723,12 @@
             dma((RANKS,)),
         ],
         compiler_params=pltpu.CompilerParams(
-            collective_id=1, has_side_effects=True, vmem_limit_bytes=VMEM_LIMIT
+            collective_id=1, has_side_effects=True, vmem_limit_bytes=RETURN_LIMIT
         ),
         cost_estimate=pl.CostEstimate(
             flops=5 * 10**9, bytes_accessed=8 * 2**20, transcendentals=0
         ),
-    )(far, own, payload, send_rows, counts, halo_rows)
+    )(far, payload, send_rows, counts, halo_rows)
 
 
 def per_device(
@@ -736,7 +763,8 @@
         w_second,
         norm_gain.reshape(1, TILE),
     )
-    grad_latent, sums = give_back(far, own, payload, send_rows, counts, halo_rows)
+    returned, sums = give_back(far, payload, send_rows, counts, halo_rows)
+    grad_latent = own + jnp.concatenate([returned[:, :TILE], returned[:, TILE:]], axis=0)
     return (
         new_edge[None, None],
         aggregate[None, None],

time: 155 us -> 107 us (0.69); the launches traced: 152 us -> 106 us
  Pallas kernels: 144 us -> 98.4 us
  local copies, waits for them, and re-layouts: 7.32 us -> 5.69 us
  other arithmetic: 0 us -> 1.56 us
    pallas_call x1, Pallas kernels: 68.4 us -> 39.7 us  [edge_pass(): pl.pallas_call(edge_kernel, name='edge_block', grid_spec=pltpu.PrefetchSc...]
    pallas_call x1, Pallas kernels: 47.6 us -> 33.6 us  [give_back(): pl.pallas_call(return_kernel, name='return_rows', out_shape=(jax.ShapeDty...]
    pallas_call x1, Pallas kernels: 28 us -> 25.2 us  [fetch(): pl.pallas_call(fetch_kernel, name='fetch_rows', out_shape=(jax.ShapeDtype...]
    broadcast_in_dim x0 -> x1, other arithmetic: none -> 1.56 us  [per_device(): grad_latent[None, None]]
    unnamed x1 -> x12, local copies, waits for them, and re-layouts: 3.04 us -> 3.72 us
where the time goes in v2:
time: 107 us; the launch traced here: 106 us
  Pallas kernels  98.4 us (92%)
  local copies, waits for them, and re-layouts  5.69 us (5%)
  other arithmetic  1.56 us (1%)
    pallas_call x1, Pallas kernels, edge_pass(): pl.pallas_call(edge_kernel, name='edge_block', grid_spec=pltpu.PrefetchSc...  39.7 us
    pallas_call x1, Pallas kernels, give_back(): pl.pallas_call(return_kernel, name='return_rows', out_shape=(jax.ShapeDty...  33.6 us
    pallas_call x1, Pallas kernels, fetch(): pl.pallas_call(fetch_kernel, name='fetch_rows', out_shape=(jax.ShapeDtype...  25.2 us
    unnamed x12, local copies, waits for them, and re-layouts  3.72 us

profile of v2, /device:TPU:1, one launch (start us, length us, event | category | flops | bytes accessed | tf_op | source)
XLA Modules:
  0.0 106.4 jit_solution(15199668413849108996)
XLA Ops:
  0.6 25.2 %fetch_rows.1 = (bf16[68,128,128]{2,1,0:T(8,128)(2,1)}, s32[2,128]{1,0:T(2,128)}) custom-call(bf16[4096,128]{1,0:T(8,128)(2,1)} %bitcast.26, s32[4,128]{1,0:T(4,128)} %bitcast.19, s32[4]{0:T(128)} %bitcast.21, s32[4,1024]{1,0:T(4,128)} %bitcast.17, s32[128,128]{1,0:T(8,128)} %bitcast.27, s32[128,128]{1,0:T(8,128)} %bitcast.29), custom_call_target="tpu_custom_call" | custom-call | flops 5000000000 | bytes 8388608 | tf_op jit(solution)/shard_map/fetch_rows/pallas_call | solution.py:229
  25.8 0.0 copy-start
  25.9 0.0 copy-start.1
  25.9 0.0 copy-start.2
  25.9 39.7 %edge_block.1 = (bf16[16384,128]{1,0:T(8,128)(2,1)}, bf16[16384,128]{1,0:T(8,128)(2,1)}, bf16[4608,128]{1,0:T(8,128)(2,1)}, bf16[36,128,128]{2,1,0:T(8,128)(2,1)...) custom-call(s32[2,128]{1,0:T(2,128)} %get-tuple-element.17.meta_ref, bf16[16384,128]{1,0:T(8,128)(2,1)} %bitcast.23, ...), custom_call_target="tpu_custom_call" | custom-call | flops 12000000000 | bytes 25165824 | tf_op jit(solution)/shard_map/edge_block/pallas_call | solution.py:445
  65.5 0.0 copy-done
  65.5 0.0 copy-done.1
  65.6 0.0 copy-done.2
  65.6 0.0 copy-start.3
  65.6 1.3 %copy-done.3 = bf16[36,128,128]{2,1,0:T(8,128)(2,1)S(1)} copy-done((bf16[36,128,128]{2,1,0:T(8,128)(2,1)S(1)}, bf16[36,128,128]{2,1,0:T(8,128)(2,1)}, u32[]{:S(2)}) %copy-start.3) | copy-done | bytes 1179672
  66.8 0.0 copy-start.4
  66.8 1.0 copy-done.4
  67.8 33.6 %return_rows.1 = (f32[2048,256]{1,0:T(8,128)S(1)}, f32[520,128]{1,0:T(8,128)S(1)}) custom-call(bf16[36,128,128]{2,1,0:T(8,128)(2,1)S(1)} %copy-done.3, f32[32,24,128]{2,1,0:T(8,128)S(1)} %copy-done.4, s32[4,128]{1,0:T(4,128)S(1)} %bitcast.20, s32[4]{0:T(128)S(1)} %bitcast.22, s32[4,1024]{1,0:T(4,128)S(1)} %bitcast.18), custom_call_target="tpu_custom_call" | custom-call | flops 5000000000 | bytes 8388608 | tf_op jit(solution)/shard_map/return_rows/pallas_call | solution.py:700
  101.4 0.0 copy-start.5
  101.4 0.1 fusion.1
  101.6 1.4 %copy-done.5 = f32[4096,128]{1,0:T(8,128)S(1)} copy-done((f32[4096,128]{1,0:T(8,128)S(1)}, f32[4096,128]{1,0:T(8,128)}, u32[]{:S(2)}) %copy-start.5) | copy-done | bytes 2097176
  103.0 1.6 %fusion = f32[1,1,4096,128]{3,2,1,0:T(8,128)} fusion(f32[4096,128]{1,0:T(8,128)S(1)} %copy-done.5, f32[2048,128]{1,0:T(8,128)S(1)} %get-tuple-element.28, f32[2048,128]{1,0:T(8,128)S(1)} %get-tuple-element.27), kind=kLoop, calls=%fused_computation.1 | loop fusion | flops 1048576 | bytes 6291456 | tf_op jit(solution)/shard_map/broadcast_in_dim | solution.py:772
  104.6 0.5 slice_bitcast_fusion
  105.1 0.6 slice.18
  105.7 0.7 slice.17
Async XLA Ops:
  25.8 39.7 %copy-start = (s32[1,1,4,1024]{3,2,1,0:T(4,128)S(1)}, s32[1,1,4,1024]{3,2,1,0:T(4,128)}, u32[]{:S(2)}) copy-start(s32[1,1,4,1024]{3,2,1,0:T(4,128)} %param.19) | copy-start | bytes 49156
  25.9 39.7 %copy-start.1 = (s32[1,1,4,128]{3,2,1,0:T(4,128)S(1)}, s32[1,1,4,128]{3,2,1,0:T(4,128)}, u32[]{:S(2)}) copy-start(s32[1,1,4,128]{3,2,1,0:T(4,128)} %param.17) | copy-start | bytes 6148
  25.9 39.7 %copy-start.2 = (s32[1,1,4]{2,1,0:T(1,128)S(1)}, s32[1,1,4]{2,1,0:T(1,128)}, u32[]{:S(2)}) copy-start(s32[1,1,4]{2,1,0:T(1,128)} %param.18) | copy-start | bytes 52
  65.6 1.3 %copy-start.3 = (bf16[36,128,128]{2,1,0:T(8,128)(2,1)S(1)}, bf16[36,128,128]{2,1,0:T(8,128)(2,1)}, u32[]{:S(2)}) copy-start(bf16[36,128,128]{2,1,0:T(8,128)(2,1)} %get-tuple-element.23.far_ref) | copy-start | bytes 3538948
  66.8 1.0 copy-start.4
  101.4 1.6 %copy-start.5 = (f32[4096,128]{1,0:T(8,128)S(1)}, f32[4096,128]{1,0:T(8,128)}, u32[]{:S(2)}) copy-start(f32[4096,128]{1,0:T(8,128)} %get-tuple-element.22) | copy-start | bytes 6291460

commit v3 on v2

--- a/solution.py
+++ b/solution.py
@@ -29,6 +29,7 @@
 CHUNK = 24
 VMEM_LIMIT = 62 * 2**20
 RETURN_LIMIT = 24 * 2**20
+EDGE_LIMIT = 48 * 2**20
 WEIGHT_CHUNK = 16
 
 
@@ -115,9 +116,10 @@
 
 
 def fetch_kernel(
-    lat_ref, send_ref, count_ref, halo_ref, snd_ref, rcv_ref,
-    tab_ref, meta_ref,
-    lat_t, out_buf, zero_buf, send_sem, recv_sem, own_sem, zero_sem,
+    lat_ref, send_ref, count_ref, halo_ref, snd_ref, rcv_ref, w1_ref, cota_ref,
+    tab_ref, ps_ref, pr_ref, ca_ref, meta_ref,
+    lat_t, out_buf, far_in, ps_buf, pr_buf, ca_buf,
+    send_sem, recv_sem, tab_sem, ps_sem, own_sem,
 ):
     barrier = pltpu.get_barrier_semaphore()
     greet_neighbours(barrier)
@@ -127,30 +129,10 @@
         lat_t[b] = rows.T
         return 0
 
-    lax.fori_loop(0, OWN_BLOCKS, turn, 0, unroll=4)
-    own_copy = pltpu.make_async_copy(lat_t, tab_ref.at[pl.ds(0, OWN_BLOCKS)], own_sem)
-    own_copy.start()
-    zero_buf[...] = jnp.zeros_like(zero_buf)
+    lax.fori_loop(0, OWN_BLOCKS, turn, 0, unroll=8)
+    own_tab = pltpu.make_async_copy(lat_t, tab_ref.at[pl.ds(0, OWN_BLOCKS)], own_sem.at[0])
+    own_tab.start()
     half = OWN_BLOCKS // 2
-
-    def zero_copies(k):
-        return [
-            pltpu.make_async_copy(
-                zero_buf.at[pl.ds(0, count)],
-                tab_ref.at[pl.ds(OWN_BLOCKS + table_place(k, at), count)],
-                zero_sem.at[k, run],
-            )
-            for run, (at, count) in enumerate(RUNS[k])
-        ]
-
-    for k in (2, 3):
-        _, exists = neighbour(k)
-
-        def fill(k=k):
-            for copy in zero_copies(k):
-                copy.start()
-
-        pl.when(jnp.logical_not(exists))(fill)
 
     def pick(index):
         low = jnp.where(index >= HALF, index - HALF, index)
@@ -182,10 +164,6 @@
 
     pl.semaphore_wait(barrier, neighbour_count())
 
-    def start(k, run):
-        copy, exists = far_copy(out_buf, tab_ref, send_sem, recv_sem, k, run, OWN_BLOCKS, k ^ 1)
-        guarded(exists, copy.start)
-
     for k, run in ORDER:
         at, count = RUNS[k][run]
         if at:
@@ -199,50 +177,131 @@
                 return 0
 
             lax.fori_loop(0, count // 2, gather, 0)
-        start(k, run)
+        copy, exists = far_copy(out_buf, far_in, send_sem, recv_sem, k, run, 0, k ^ 1)
+        guarded(exists, copy.start)
+
+    for k in (2, 3):
+        _, exists = neighbour(k)
+
+        def fill(k=k):
+            for at, count in RUNS[k]:
+                first = table_place(k, at)
+                far_in[first : first + count] = jnp.zeros((count, TILE, TILE), BF16)
+
+        pl.when(jnp.logical_not(exists))(fill)
 
     firsts = lax.shift_right_logical(
         jnp.concatenate([snd_ref[...].T[:1], rcv_ref[...].T[:1]], axis=0), 7
     )
     meta_ref[...] = firsts
-
-    own_copy.wait()
-    for k in (2, 3):
-        _, exists = neighbour(k)
-
-        def drain(k=k):
-            for copy in zero_copies(k):
-                copy.wait()
-
-        pl.when(jnp.logical_not(exists))(drain)
+    ws_t = w1_ref[TILE : 2 * TILE, :].T
+    both_t = jnp.concatenate([ws_t, w1_ref[2 * TILE :, :].T], axis=0)
+
+    def turn_cotangents(at, _):
+        first = at * 4
+        rows = pl.ds(pl.multiple_of(first * TILE, 4 * TILE), 4 * TILE)
+        turned = cota_ref[rows, :].T
+        for n in range(4):
+            ca_buf[first + n] = turned[:, n * TILE : (n + 1) * TILE]
+        return 0
+
+    lax.fori_loop(0, OWNED_BLOCKS // 4, turn_cotangents, 0)
+    own_ca = pltpu.make_async_copy(ca_buf, ca_ref, own_sem.at[1])
+    own_ca.start()
+
+    def project_both(source, first, place):
+        blocks = jnp.concatenate([source[first + n] for n in range(4)], axis=1)
+        out = mm(both_t, blocks).astype(BF16)
+        for n in range(4):
+            ps_buf[place + n] = out[:TILE, n * TILE : (n + 1) * TILE]
+            pr_buf[place + n] = out[TILE:, n * TILE : (n + 1) * TILE]
+
+    def project_own(at, _):
+        project_both(lat_t, at * 4, at * 4)
+        return 0
+
+    lax.fori_loop(0, OWN_BLOCKS // 4, project_own, 0)
+    own_ps = pltpu.make_async_copy(
+        ps_buf.at[pl.ds(0, OWN_BLOCKS)], ps_ref.at[pl.ds(0, OWN_BLOCKS)], own_sem.at[2]
+    )
+    own_ps.start()
+
+    def arrived(k, run):
+        copy, exists = far_copy(out_buf, far_in, send_sem, recv_sem, k, run, 0, k)
+        guarded(exists, copy.wait_recv)
+
+    for k in range(4):
+        arrived(k, 0)
+    project_both(far_in, 0, OWN_BLOCKS)
+    own_pr = pltpu.make_async_copy(pr_buf, pr_ref, own_sem.at[3])
+    own_pr.start()
+    mig_ps = pltpu.make_async_copy(
+        ps_buf.at[pl.ds(OWN_BLOCKS, MIG_BLOCKS)], ps_ref.at[pl.ds(OWN_BLOCKS, MIG_BLOCKS)],
+        own_sem.at[4],
+    )
+    mig_ps.start()
+    mig_tab = pltpu.make_async_copy(
+        far_in.at[pl.ds(0, MIG_BLOCKS)], tab_ref.at[pl.ds(OWN_BLOCKS, MIG_BLOCKS)], own_sem.at[5]
+    )
+    mig_tab.start()
+    copies = [own_tab, own_ca, own_ps, own_pr, mig_ps, mig_tab]
+
+    for k, run in ORDER[4:]:
+        at, count = RUNS[k][run]
+        arrived(k, run)
+        first = table_place(k, at)
+        place = OWN_BLOCKS + first
+        tab_copy = pltpu.make_async_copy(
+            far_in.at[pl.ds(first, count)], tab_ref.at[pl.ds(place, count)], tab_sem.at[k, run]
+        )
+        tab_copy.start()
+        blocks = jnp.concatenate([far_in[first + n] for n in range(count)], axis=1)
+        out = mm(ws_t, blocks).astype(BF16)
+        for n in range(count):
+            ps_buf[place + n] = out[:, n * TILE : (n + 1) * TILE]
+        ps_copy = pltpu.make_async_copy(
+            ps_buf.at[pl.ds(place, count)], ps_ref.at[pl.ds(place, count)], ps_sem.at[k, run]
+        )
+        ps_copy.start()
+        copies += [tab_copy, ps_copy]
+
     for k, run in ORDER:
-        copy, exists = far_copy(out_buf, tab_ref, send_sem, recv_sem, k, run, OWN_BLOCKS, k ^ 1)
+        copy, exists = far_copy(out_buf, far_in, send_sem, recv_sem, k, run, 0, k ^ 1)
         guarded(exists, copy.wait_send)
-        back, exists = far_copy(out_buf, tab_ref, send_sem, recv_sem, k, run, OWN_BLOCKS, k)
-        guarded(exists, back.wait_recv)
-
-
-def fetch(nodes, send_rows, counts, halo_rows, send_idx, recv_idx):
+    for copy in copies:
+        copy.wait()
+
+
+def fetch(nodes, send_rows, counts, halo_rows, send_idx, recv_idx, w_first, cot_agg):
     vmem = pl.BlockSpec(memory_space=pltpu.VMEM)
     smem = pl.BlockSpec(memory_space=pltpu.SMEM)
+    hbm = pl.BlockSpec(memory_space=pl.ANY)
+    dma = pltpu.SemaphoreType.DMA
     block = (TILE, TILE)
     return pl.pallas_call(
         fetch_kernel,
         name="fetch_rows",
         out_shape=(
             jax.ShapeDtypeStruct((TABLE_BLOCKS,) + block, BF16),
+            jax.ShapeDtypeStruct((TABLE_BLOCKS,) + block, BF16),
+            jax.ShapeDtypeStruct((OWNED_BLOCKS,) + block, BF16),
+            jax.ShapeDtypeStruct((OWNED_BLOCKS,) + block, BF16),
             jax.ShapeDtypeStruct((2, TILE), jnp.int32),
         ),
-        in_specs=[vmem, vmem, smem, vmem, vmem, vmem],
-        out_specs=(pl.BlockSpec(memory_space=pl.ANY), vmem),
+        in_specs=[vmem, vmem, smem, vmem, vmem, vmem, vmem, vmem],
+        out_specs=(hbm, hbm, hbm, hbm, vmem),
         scratch_shapes=[
             pltpu.VMEM((OWN_BLOCKS,) + block, BF16),
             pltpu.VMEM((FAR_BLOCKS,) + block, BF16),
-            pltpu.VMEM((LONGEST,) + block, BF16),
-            pltpu.SemaphoreType.DMA((4, MOST_RUNS)),
-            pltpu.SemaphoreType.DMA((4, MOST_RUNS)),
-            pltpu.SemaphoreType.DMA,
-            pltpu.SemaphoreType.DMA((4, MOST_RUNS)),
+            pltpu.VMEM((FAR_BLOCKS,) + block, BF16),
+            pltpu.VMEM((TABLE_BLOCKS,) + block, BF16),
+            pltpu.VMEM((OWNED_BLOCKS,) + block, BF16),
+            pltpu.VMEM((OWNED_BLOCKS,) + block, BF16),
+            dma((4, MOST_RUNS)),
+            dma((4, MOST_RUNS)),
+            dma((4, MOST_RUNS)),
+            dma((4, MOST_RUNS)),
+            dma((6,)),
         ],
         compiler_params=pltpu.CompilerParams(
             collective_id=0, has_side_effects=True, vmem_limit_bytes=VMEM_LIMIT
@@ -250,22 +309,24 @@
         cost_estimate=pl.CostEstimate(
             flops=5 * 10**9, bytes_accessed=8 * 2**20, transcendentals=0
         ),
-    )(nodes, send_rows, counts, halo_rows, send_idx, recv_idx)
+    )(nodes, send_rows, counts, halo_rows, send_idx, recv_idx, w_first, cot_agg)
 
 
 def edge_kernel(
-    meta_ref, edge_ref, cot_ref, snd_ref, rcv_ref, tab_ref, cota_ref,
+    meta_ref, edge_ref, cot_ref, snd_ref, rcv_ref, tab_hbm, ps_t, pr_t, ca_t,
     w1_ref, w2_ref, gain_ref,
     new_ref, grad_ref, agg_ref, far_ref, own_ref, pay_ref,
-    ps_t, pr_t, ca_t, s_acc, ra_acc, fe_acc, w2_acc, g_acc, gain_b, w1_t, w2_t, fsr_acc,
+    tab_ref, s_acc, ra_acc, fe_acc, w2_acc, g_acc, gain_b, w1_t, w2_t, fsr_acc, tab_sem,
 ):
     step = pl.program_id(0)
     steps = pl.num_programs(0)
 
+    tab_copy = pltpu.make_async_copy(tab_hbm, tab_ref, tab_sem)
+
     @pl.when(step == 0)
     def _prologue():
-        for part in range(3):
-            w1_t[part] = w1_ref[part * TILE : (part + 1) * TILE, :].T
+        tab_copy.start()
+        w1_t[...] = w1_ref[:TILE, :].T
         w2_t[...] = w2_ref[...].T
         gain_b[...] = jnp.broadcast_to(gain_ref[...], (TILE, TILE)).T
 
@@ -284,31 +345,8 @@
         w2_acc[...] = jnp.zeros_like(w2_acc)
         g_acc[...] = jnp.zeros_like(g_acc)
 
-        def project(at, _):
-            first = at * 4
-            blocks = jnp.concatenate([tab_ref[first + n] for n in range(4)], axis=1)
-            out = mm(w1_t[1], blocks).astype(BF16)
-            for n in range(4):
-                ps_t[first + n] = out[:, n * TILE : (n + 1) * TILE]
-            return 0
-
-        lax.fori_loop(0, TABLE_BLOCKS // 4, project, 0)
-
-        def project_owned(at, _):
-            first = at * 4
-            blocks = jnp.concatenate([tab_ref[first + n] for n in range(4)], axis=1)
-            out = mm(w1_t[2], blocks).astype(BF16)
-            rows = pl.ds(pl.multiple_of(first * TILE, 4 * TILE), 4 * TILE)
-            turned = cota_ref[rows, :].T
-            for n in range(4):
-                pr_t[first + n] = out[:, n * TILE : (n + 1) * TILE]
-                ca_t[first + n] = turned[:, n * TILE : (n + 1) * TILE]
-            return 0
-
-        lax.fori_loop(0, OWNED_BLOCKS // 4, project_owned, 0)
-
     we = w1_ref[:TILE, :]
-    we_t = w1_t[0]
+    we_t = w1_t[...]
     w2 = w2_ref[...]
     gain = jnp.concatenate([gain_b[...]] * GROUP, axis=1)
     wide = GROUP * TILE
@@ -318,7 +356,6 @@
         first = pl.multiple_of(p * wide, wide)
         rows = pl.ds(first, wide)
         edges = edge_ref[rows, :]
-        edges_t = edges.T
         cot_t = cot_ref[rows, :].T.astype(F32)
         hot_s, hot_r, near, cots, blocks = [], [], [], [], []
         for side in range(GROUP):
@@ -336,7 +373,7 @@
                 )
             )
             cots.append(mm(ca_t[br], hr))
-        preact = mm(we_t, edges_t) + jnp.concatenate(near, axis=1)
+        preact = mmt(we_t, edges) + jnp.concatenate(near, axis=1)
         sig = 0.5 * jnp.tanh(0.5 * preact) + 0.5
         hidden = preact * sig
         slope = sig + hidden * (1.0 - sig)
@@ -347,9 +384,8 @@
         inverse = lax.rsqrt(variance + EPS)
         normed = centred * inverse
         message = normed * gain
-        new_edge = (edges_t.astype(F32) + message).astype(BF16)
-        new_ref[rows, :] = new_edge.T
         message = message.astype(BF16)
+        new_ref[rows, :] = (edges.astype(F32) + message.T.astype(F32)).astype(BF16)
         d_message = cot_t + jnp.concatenate(cots, axis=1)
         weighted = d_message * normed
         g_sum = weighted[:, :TILE]
@@ -363,8 +399,8 @@
         w2_acc[...] += mmt(hidden, d_output)
         d_preact = (mm(w2, d_output) * slope).astype(BF16)
         fe_acc[...] += mm(d_preact, edges)
-        grad_edge = (cot_t + mm(we, d_preact)).astype(BF16)
-        grad_ref[rows, :] = grad_edge.T
+        d_edge = mm(we, d_preact).astype(BF16)
+        grad_ref[rows, :] = (cot_ref[rows, :].astype(F32) + d_edge.T.astype(F32)).astype(BF16)
         for side in range(GROUP):
             bs, br = blocks[side]
             lanes = slice(side * TILE, (side + 1) * TILE)
@@ -378,6 +414,7 @@
 
     @pl.when(step == steps - 1)
     def _epilogue():
+        tab_copy.wait()
         ws = w1_ref[TILE : 2 * TILE, :]
         wr = w1_ref[2 * TILE :, :]
         wsr = jnp.concatenate([ws, wr], axis=1)
@@ -398,7 +435,7 @@
 
         def own(at, _):
             rows, both = owned(at)
-            own_ref[rows, :] = mmt(both, wsr)
+            own_ref[rows, :] = both
             return 0
 
         lax.fori_loop(0, OWN_BLOCKS // 4, own, 0)
@@ -433,7 +470,9 @@
                 pay_ref[n * per + c, WEIGHT_CHUNK:, :] = g_tile
 
 
-def edge_pass(meta, edges, cot_edge, send_idx, recv_idx, table, cot_agg, w_first, w_second, gain):
+def edge_pass(
+    meta, edges, cot_edge, send_idx, recv_idx, table, ps, pr, ca, w_first, w_second, gain
+):
     rows = GROUPS * GROUP * TILE
     steps = edges.shape[0] // rows
     block = (TILE, TILE)
@@ -453,8 +492,10 @@
                 stream,
                 whole(*send_idx.shape),
                 whole(*recv_idx.shape),
-                whole(*table.shape),
-                whole(*cot_agg.shape),
+                pl.BlockSpec(memory_space=pl.ANY),
+                whole(*ps.shape),
+                whole(*pr.shape),
+                whole(*ca.shape),
                 whole(*w_first.shape),
                 whole(*w_second.shape),
                 whole(*gain.shape),
@@ -464,22 +505,21 @@
                 stream,
                 whole(OWNED_BLOCKS * TILE, TILE),
                 whole(FAR_BLOCKS, TILE, TILE),
-                whole(OWN_BLOCKS * TILE, TILE),
+                whole(OWN_BLOCKS * TILE, 2 * TILE),
                 whole(RANKS, CHUNK, TILE),
             ],
             scratch_shapes=[
                 pltpu.VMEM((TABLE_BLOCKS,) + block, BF16),
-                pltpu.VMEM((OWNED_BLOCKS,) + block, BF16),
-                pltpu.VMEM((OWNED_BLOCKS,) + block, BF16),
                 pltpu.VMEM((TABLE_BLOCKS,) + block, F32),
                 pltpu.VMEM((OWNED_BLOCKS, TILE, 2 * TILE), F32),
                 pltpu.VMEM(block, F32),
                 pltpu.VMEM(block, F32),
                 pltpu.VMEM(block, F32),
                 pltpu.VMEM(block, F32),
-                pltpu.VMEM((3,) + block, BF16),
+                pltpu.VMEM(block, BF16),
                 pltpu.VMEM(block, BF16),
                 pltpu.VMEM((TILE, 2 * TILE), F32),
+                pltpu.SemaphoreType.DMA,
             ],
         ),
         out_shape=[
@@ -487,14 +527,14 @@
             jax.ShapeDtypeStruct(edges.shape, BF16),
             jax.ShapeDtypeStruct((OWNED_BLOCKS * TILE, TILE), BF16),
             jax.ShapeDtypeStruct((FAR_BLOCKS, TILE, TILE), BF16),
-            jax.ShapeDtypeStruct((OWN_BLOCKS * TILE, TILE), F32),
+            jax.ShapeDtypeStruct((OWN_BLOCKS * TILE, 2 * TILE), BF16),
             jax.ShapeDtypeStruct((RANKS, CHUNK, TILE), F32),
         ],
-        compiler_params=pltpu.CompilerParams(vmem_limit_bytes=VMEM_LIMIT),
+        compiler_params=pltpu.CompilerParams(vmem_limit_bytes=EDGE_LIMIT),
         cost_estimate=pl.CostEstimate(
             flops=12 * 10**9, bytes_accessed=24 * 2**20, transcendentals=3 * 2**20
         ),
-    )(meta, edges, cot_edge, send_idx, recv_idx, table, cot_agg, w_first, w_second, gain)
+    )(meta, edges, cot_edge, send_idx, recv_idx, table, ps, pr, ca, w_first, w_second, gain)
 
 
 def rank_device(rank):
@@ -524,9 +564,9 @@
 
 
 def return_kernel(
-    far_ref, pay_ref, send_ref, count_ref, halo_ref,
-    acc, sum_ref,
-    back, mine, ring, col, got, pay_sem,
+    far_ref, own_ref, pay_ref, send_ref, count_ref, halo_ref, w1_ref,
+    lat_ref, sum_ref,
+    back, own_buf, mine, ring, col, got, pay_sem, own_sem,
     send_sem, recv_sem, rs_send, rs_recv, col_send, col_recv, ag_send, ag_recv,
 ):
     rank = my_rank()
@@ -546,7 +586,8 @@
 
     pay_copy = pltpu.make_async_copy(pay_ref.at[rank], ring.at[rank], pay_sem)
     pay_copy.start()
-    acc[...] = jnp.zeros_like(acc)
+    own_copy = pltpu.make_async_copy(own_ref, own_buf, own_sem)
+    own_copy.start()
     pl.semaphore_wait(barrier, neighbour_count() + RANKS - 1 + 3)
 
     def give(k, run, to_slot):
@@ -580,6 +621,15 @@
         scatter_copy(s).wait()
         return 0
 
+    own_copy.wait()
+    wsr = jnp.concatenate([w1_ref[TILE : 2 * TILE, :], w1_ref[2 * TILE :, :]], axis=1)
+
+    def own_part(m, _):
+        rows = pl.ds(pl.multiple_of(m * 4 * TILE, 4 * TILE), 4 * TILE)
+        lat_ref[rows, :] = mmt(own_buf[rows, :], wsr)
+        return 0
+
+    lax.fori_loop(0, OWN_BLOCKS // 4, own_part, 0, unroll=2)
     lax.fori_loop(1, RANKS, wait_scatter, 0)
 
     pay_copy.wait()
@@ -617,7 +667,9 @@
         def piece(m, _):
             first = pl.multiple_of(m * 2 * TILE, 2 * TILE)
             hot = onehot(2 * TILE, low, first)
-            acc[pl.ds(first, 2 * TILE), :] += mm(hot, right)
+            part = mm(hot, right)
+            lat_ref[pl.ds(first, 2 * TILE), :] += part[:, :TILE]
+            lat_ref[pl.ds(HALF + first, 2 * TILE), :] += part[:, TILE:]
             return 0
 
         lax.fori_loop(0, HALF // (2 * TILE), piece, 0, unroll=8)
@@ -692,7 +744,7 @@
         sum_ref[c * WEIGHT_CHUNK : (c + 1) * WEIGHT_CHUNK, :] = got[c]
 
 
-def give_back(far, payload, send_rows, counts, halo_rows):
+def give_back(far, own, payload, send_rows, counts, halo_rows, w_first):
     vmem = pl.BlockSpec(memory_space=pltpu.VMEM)
     smem = pl.BlockSpec(memory_space=pltpu.SMEM)
     hbm = pl.BlockSpec(memory_space=pl.ANY)
@@ -701,17 +753,19 @@
         return_kernel,
         name="return_rows",
         out_shape=(
-            jax.ShapeDtypeStruct((HALF, 2 * TILE), F32),
+            jax.ShapeDtypeStruct((OWN_BLOCKS * TILE, TILE), F32),
             jax.ShapeDtypeStruct((RANKS * WEIGHT_CHUNK + CHUNK - WEIGHT_CHUNK, TILE), F32),
         ),
-        in_specs=[hbm, hbm, vmem, smem, vmem],
+        in_specs=[hbm, hbm, hbm, vmem, smem, vmem, vmem],
         out_specs=(vmem, vmem),
         scratch_shapes=[
             pltpu.VMEM((FAR_BLOCKS, TILE, TILE), BF16),
+            pltpu.VMEM((OWN_BLOCKS * TILE, 2 * TILE), BF16),
             pltpu.VMEM((WEIGHT_CHUNK, TILE), F32),
             pltpu.VMEM((RANKS, CHUNK, TILE), F32),
             pltpu.VMEM((4, CHUNK, TILE), F32),
             pltpu.VMEM((RANKS, WEIGHT_CHUNK, TILE), F32),
+            dma,
             dma,
             dma((4, MOST_RUNS)),
             dma((4, MOST_RUNS)),
@@ -728,7 +782,7 @@
         cost_estimate=pl.CostEstimate(
             flops=5 * 10**9, bytes_accessed=8 * 2**20, transcendentals=0
         ),
-    )(far, payload, send_rows, counts, halo_rows)
+    )(far, own, payload, send_rows, counts, halo_rows, w_first)
 
 
 def per_device(
@@ -750,7 +804,9 @@
     counts = send_count[0, 0]
     send_idx = senders.reshape(-1, TILE)
     recv_idx = receivers.reshape(-1, TILE)
-    table, meta = fetch(latent[0, 0], send_rows, counts, halo_rows, send_idx, recv_idx)
+    table, ps, pr, ca, meta = fetch(
+        latent[0, 0], send_rows, counts, halo_rows, send_idx, recv_idx, w_first, cotangent_agg[0, 0]
+    )
     new_edge, grad_edge, aggregate, far, own, payload = edge_pass(
         meta,
         edge_state[0, 0],
@@ -758,13 +814,14 @@
         send_idx,
         recv_idx,
         table,
-        cotangent_agg[0, 0],
+        ps,
+        pr,
+        ca,
         w_first,
         w_second,
         norm_gain.reshape(1, TILE),
     )
-    returned, sums = give_back(far, payload, send_rows, counts, halo_rows)
-    grad_latent = own + jnp.concatenate([returned[:, :TILE], returned[:, TILE:]], axis=0)
+    grad_latent, sums = give_back(far, own, payload, send_rows, counts, halo_rows, w_first)
     return (
         new_edge[None, None],
         aggregate[None, None],

time: 107 us -> 101 us (0.944)
  Pallas kernels: 98.4 us -> 91.9 us
  local copies, waits for them, and re-layouts: 5.69 us -> 7.98 us
  other arithmetic: 1.56 us -> 0 us
    pallas_call x1, Pallas kernels: 39.7 us -> 31.7 us  [edge_pass(): pl.pallas_call(edge_kernel, name='edge_block', grid_spec=pltpu.PrefetchSc...]
    unnamed x12 -> x25, local copies, waits for them, and re-layouts: 3.72 us -> 6.15 us
    broadcast_in_dim x1 -> x0, other arithmetic: 1.56 us -> none  [per_device(): grad_latent[None, None]]
where the time goes in v3:
time: 101 us
  Pallas kernels  91.9 us (91%)
  local copies, waits for them, and re-layouts  7.98 us (8%)
    pallas_call x1, Pallas kernels, give_back(): pl.pallas_call(return_kernel, name='return_rows', out_shape=(jax.ShapeDty...  34.2 us
    pallas_call x1, Pallas kernels, edge_pass(): pl.pallas_call(edge_kernel, name='edge_block', grid_spec=pltpu.PrefetchSc...  31.7 us
    pallas_call x1, Pallas kernels, fetch(): pl.pallas_call(fetch_kernel, name='fetch_rows', out_shape=(jax.ShapeDtype...  25.9 us
    unnamed x25, local copies, waits for them, and re-layouts  6.15 us

profile of v3, /device:TPU:1, one launch (start us, length us, event | category | flops | bytes accessed | tf_op | source)
XLA Modules:
  0.0 100.6 jit_solution(3242459782006767335)
XLA Ops:
  0.6 0.0 copy-start
  0.6 0.0 copy-start.1
  0.7 0.0 copy-start.2
  0.7 0.0 copy-start.3
  0.7 0.0 copy-start.6
  0.7 25.9 %fetch_rows.1 = (bf16[68,128,128]{2,1,0:T(8,128)(2,1)}, bf16[68,128,128]{2,1,0:T(8,128)(2,1)}, bf16[36,128,128]{2,1,0:T(8,128)(2,1)}, bf16[36,128,128]{2,1,0:T(8,128)(2,1)}, s32[2,128]{1,0:T(2,128)}) custom-call(bf16[4096,128]{1,0:T(8,128)(2,1)} %bitcast.31, s32[4,128]{1,0:T(4,128)} %bitcast.23, s32[4]{0:T(128)} %bitcast.26, s32[4,1024]{1,0:T(4,128)} %bitcast.21, ...), custom_call_target="tpu_custom_call" | custom-call | flops 5000000000 | bytes 8388608 | tf_op jit(solution)/shard_map/fetch_rows/pallas_call | solution.py:281
  26.6 0.0 copy-done
  26.6 0.0 copy-done.1
  26.6 0.0 copy-done.2
  26.6 0.0 copy-done.3
  26.6 0.0 copy-done.6
  26.6 0.0 copy-start.9
  26.7 1.3 %copy-done.9 = bf16[36,128,128]{2,1,0:T(8,128)(2,1)S(1)} copy-done((bf16[36,128,128]{2,1,0:T(8,128)(2,1)S(1)}, bf16[36,128,128]{2,1,0:T(8,128)(2,1)}, u32[]{:S(2)}) %copy-start.9) | copy-done | bytes 1179672
  27.9 0.0 copy-start.10
  27.9 1.3 %copy-done.10 = bf16[36,128,128]{2,1,0:T(8,128)(2,1)S(1)} copy-done((bf16[36,128,128]{2,1,0:T(8,128)(2,1)S(1)}, bf16[36,128,128]{2,1,0:T(8,128)(2,1)}, u32[]{:S(2)}) %copy-start.10) | copy-done | bytes 1179672
  29.2 0.0 copy-start.11
  29.2 0.7 copy-done.11
  29.9 0.0 copy-start.4
  29.9 0.0 copy-start.5
  29.9 0.0 copy-start.7
  29.9 31.7 %edge_block.1 = (bf16[16384,128]{1,0:T(8,128)(2,1)}, bf16[16384,128]{1,0:T(8,128)(2,1)}, bf16[4608,128]{1,0:T(8,128)(2,1)}, bf16[36,128,128]{2,1,0:T(8,128)(2,1)...) custom-call(s32[2,128]{1,0:T(2,128)S(1)} %copy-done.11, bf16[16384,128]{1,0:T(8,128)(2,1)} %bitcast.28, ...), custom_call_target="tpu_custom_call" | custom-call | flops 12000000000 | bytes 25165824 | tf_op jit(solution)/shard_map/edge_block/pallas_call | solution.py:484
  61.6 0.0 copy-done.4
  61.6 0.0 copy-done.5
  61.6 0.0 copy-done.7
  61.6 0.0 copy-start.8
  61.6 1.6 %copy-done.8 = bf16[4096,256]{1,0:T(8,128)(2,1)S(1)} copy-done((bf16[4096,256]{1,0:T(8,128)(2,1)S(1)}, bf16[4096,256]{1,0:T(8,128)(2,1)}, u32[]{:S(2)}) %copy-start.8) | copy-done | bytes 2097176
  63.2 34.2 %return_rows.1 = (f32[4096,128]{1,0:T(8,128)S(1)}, f32[520,128]{1,0:T(8,128)S(1)}) custom-call(bf16[36,128,128]{2,1,0:T(8,128)(2,1)S(1)} %get-tuple-element.28.far_ref, bf16[4096,256]{1,0:T(8,128)(2,1)S(1)} %copy-done.8, f32[32,24,128]{2,1,0:T(8,128)S(1)} %get-tuple-element.30.pay_ref, s32[4,128]{1,0:T(4,128)S(1)} %bitcast.24, s32[4]{0:T(128)S(1)} %bitcast.27, ...), custom_call_target="tpu_custom_call" | custom-call | flops 5000000000 | bytes 8388608 | tf_op jit(solution)/shard_map/return_rows/pallas_call | solution.py:752
  97.5 0.5 slice_bitcast_fusion
  98.0 0.6 slice.10
  98.6 0.7 slice.9
  99.3 1.3 %copy.20 = f32[1,1,4096,128]{3,2,1,0:T(8,128)} copy(f32[1,1,4096,128]{3,2,1,0:T(8,128)S(1)} %bitcast.16) | data formatting | bytes 4194304
Async XLA Ops:
  0.6 26.0 %copy-start = (bf16[384,128]{1,0:T(8,128)(2,1)S(1)}, bf16[384,128]{1,0:T(8,128)(2,1)}, u32[]{:S(2)}) copy-start(bf16[384,128]{1,0:T(8,128)(2,1)} %w1_ref.5) | copy-start | bytes 294916
  0.6 26.0 %copy-start.1 = (s32[1,1,16384]{2,1,0:T(1,128)S(1)}, s32[1,1,16384]{2,1,0:T(1,128)}, u32[]{:S(2)}) copy-start(s32[1,1,16384]{2,1,0:T(1,128)} %param.20) | copy-start | bytes 196612
  0.7 26.0 %copy-start.2 = (s32[1,1,16384]{2,1,0:T(1,128)S(1)}, s32[1,1,16384]{2,1,0:T(1,128)}, u32[]{:S(2)}) copy-start(s32[1,1,16384]{2,1,0:T(1,128)} %param.21) | copy-start | bytes 196612
  0.7 26.0 %copy-start.3 = (bf16[128,128]{1,0:T(8,128)(2,1)S(1)}, bf16[128,128]{1,0:T(8,128)(2,1)}, u32[]{:S(2)}) copy-start(bf16[128,128]{1,0:T(8,128)(2,1)} %w2_ref.1) | copy-start | bytes 98308
  0.7 26.0 %copy-start.6 = (f32[128]{0:T(128)S(1)}, f32[128]{0:T(128)}, u32[]{:S(2)}) copy-start(f32[128]{0:T(128)} %param.16) | copy-start | bytes 1540
  26.6 1.3 %copy-start.9 = (bf16[36,128,128]{2,1,0:T(8,128)(2,1)S(1)}, bf16[36,128,128]{2,1,0:T(8,128)(2,1)}, u32[]{:S(2)}) copy-start(bf16[36,128,128]{2,1,0:T(8,128)(2,1)} %get-tuple-element.23.pr_t) | copy-start | bytes 3538948
  27.9 1.3 %copy-start.10 = (bf16[36,128,128]{2,1,0:T(8,128)(2,1)S(1)}, bf16[36,128,128]{2,1,0:T(8,128)(2,1)}, u32[]{:S(2)}) copy-start(bf16[36,128,128]{2,1,0:T(8,128)(2,1)} %get-tuple-element.24.ca_t) | copy-start | bytes 3538948
  29.2 0.7 copy-start.11
  29.9 31.7 %copy-start.4 = (s32[1,1,4,1024]{3,2,1,0:T(4,128)S(1)}, s32[1,1,4,1024]{3,2,1,0:T(4,128)}, u32[]{:S(2)}) copy-start(s32[1,1,4,1024]{3,2,1,0:T(4,128)} %param.19) | copy-start | bytes 49156
  29.9 31.7 %copy-start.5 = (s32[1,1,4,128]{3,2,1,0:T(4,128)S(1)}, s32[1,1,4,128]{3,2,1,0:T(4,128)}, u32[]{:S(2)}) copy-start(s32[1,1,4,128]{3,2,1,0:T(4,128)} %param.17) | copy-start | bytes 6148
  29.9 31.7 %copy-start.7 = (s32[1,1,4]{2,1,0:T(1,128)S(1)}, s32[1,1,4]{2,1,0:T(1,128)}, u32[]{:S(2)}) copy-start(s32[1,1,4]{2,1,0:T(1,128)} %param.18) | copy-start | bytes 52
  61.6 1.6 %copy-start.8 = (bf16[4096,256]{1,0:T(8,128)(2,1)S(1)}, bf16[4096,256]{1,0:T(8,128)(2,1)}, u32[]{:S(2)}) copy-start(bf16[4096,256]{1,0:T(8,128)(2,1)} %get-tuple-element.29.own_ref) | copy-start | bytes 6291460

commit v4 on v3

--- a/solution.py
+++ b/solution.py
@@ -334,13 +334,13 @@
             s_acc[b] = jnp.zeros((TILE, TILE), F32)
             return 0
 
-        lax.fori_loop(0, TABLE_BLOCKS, zero, 0, unroll=2)
+        lax.fori_loop(0, TABLE_BLOCKS, zero, 0, unroll=4)
 
         def zero_two(b, _):
             ra_acc[b] = jnp.zeros((TILE, 2 * TILE), F32)
             return 0
 
-        lax.fori_loop(0, OWNED_BLOCKS, zero_two, 0, unroll=2)
+        lax.fori_loop(0, OWNED_BLOCKS, zero_two, 0, unroll=4)
         fe_acc[...] = jnp.zeros_like(fe_acc)
         w2_acc[...] = jnp.zeros_like(w2_acc)
         g_acc[...] = jnp.zeros_like(g_acc)
@@ -438,7 +438,7 @@
             own_ref[rows, :] = both
             return 0
 
-        lax.fori_loop(0, OWN_BLOCKS // 4, own, 0)
+        lax.fori_loop(0, OWN_BLOCKS // 4, own, 0, unroll=4)
         _, both = owned(OWN_BLOCKS // 4)
         back = mmt(wsr, both).astype(BF16)
         for n in range(MIG_BLOCKS):
@@ -454,7 +454,7 @@
             fsr_acc[:, :TILE] += mm(tab, s)
             return 0
 
-        lax.fori_loop(0, HALO_BLOCKS // 4, halo, 0)
+        lax.fori_loop(0, HALO_BLOCKS // 4, halo, 0, unroll=4)
         first = fsr_acc[:, :TILE]
         second = fsr_acc[:, TILE:]
         edge_part = fe_acc[...].T

time: 101 us -> 99 us (0.980)
  Pallas kernels: 91.9 us -> 90 us
    pallas_call x1, Pallas kernels: 31.7 us -> 29.9 us  [edge_pass(): pl.pallas_call(edge_kernel, name='edge_block', grid_spec=pltpu.PrefetchSc...]
where the time goes in v4:
time: 99 us; the launch traced here: 98.7 us
  Pallas kernels  90 us (91%)
  local copies, waits for them, and re-layouts  7.98 us (8%)
    pallas_call x1, Pallas kernels, give_back(): pl.pallas_call(return_kernel, name='return_rows', out_shape=(jax.ShapeDty...  34.2 us
    pallas_call x1, Pallas kernels, edge_pass(): pl.pallas_call(edge_kernel, name='edge_block', grid_spec=pltpu.PrefetchSc...  29.9 us
    pallas_call x1, Pallas kernels, fetch(): pl.pallas_call(fetch_kernel, name='fetch_rows', out_shape=(jax.ShapeDtype...  25.9 us
    unnamed x25, local copies, waits for them, and re-layouts  6.15 us

profile of v4, /device:TPU:1, one launch (start us, length us, event | category | flops | bytes accessed | tf_op | source)
XLA Modules:
  0.0 98.7 jit_solution(17040257841627949840)
XLA Ops:
  0.6 0.0 copy-start
  0.6 0.0 copy-start.1
  0.7 0.0 copy-start.2
  0.7 0.0 copy-start.3
  0.7 0.0 copy-start.6
  0.7 25.9 %fetch_rows.1 = (bf16[68,128,128]{2,1,0:T(8,128)(2,1)}, bf16[68,128,128]{2,1,0:T(8,128)(2,1)}, bf16[36,128,128]{2,1,0:T(8,128)(2,1)}, bf16[36,128,128]{2,1,0:T(8,128)(2,1)}, s32[2,128]{1,0:T(2,128)}) custom-call(bf16[4096,128]{1,0:T(8,128)(2,1)} %bitcast.31, s32[4,128]{1,0:T(4,128)} %bitcast.23, s32[4]{0:T(128)} %bitcast.26, s32[4,1024]{1,0:T(4,128)} %bitcast.21, ...), custom_call_target="tpu_custom_call" | custom-call | flops 5000000000 | bytes 8388608 | tf_op jit(solution)/shard_map/fetch_rows/pallas_call | solution.py:281
  26.6 0.0 copy-done
  26.6 0.0 copy-done.1
  26.6 0.0 copy-done.2
  26.6 0.0 copy-done.3
  26.6 0.0 copy-done.6
  26.6 0.0 copy-start.9
  26.7 1.3 %copy-done.9 = bf16[36,128,128]{2,1,0:T(8,128)(2,1)S(1)} copy-done((bf16[36,128,128]{2,1,0:T(8,128)(2,1)S(1)}, bf16[36,128,128]{2,1,0:T(8,128)(2,1)}, u32[]{:S(2)}) %copy-start.9) | copy-done | bytes 1179672
  27.9 0.0 copy-start.10
  27.9 1.3 %copy-done.10 = bf16[36,128,128]{2,1,0:T(8,128)(2,1)S(1)} copy-done((bf16[36,128,128]{2,1,0:T(8,128)(2,1)S(1)}, bf16[36,128,128]{2,1,0:T(8,128)(2,1)}, u32[]{:S(2)}) %copy-start.10) | copy-done | bytes 1179672
  29.2 0.0 copy-start.11
  29.2 0.7 copy-done.11
  29.9 0.0 copy-start.4
  29.9 0.0 copy-start.5
  29.9 0.0 copy-start.7
  29.9 29.9 %edge_block.1 = (bf16[16384,128]{1,0:T(8,128)(2,1)}, bf16[16384,128]{1,0:T(8,128)(2,1)}, bf16[4608,128]{1,0:T(8,128)(2,1)}, bf16[36,128,128]{2,1,0:T(8,128)(2,1)...) custom-call(s32[2,128]{1,0:T(2,128)S(1)} %copy-done.11, bf16[16384,128]{1,0:T(8,128)(2,1)} %bitcast.28, ...), custom_call_target="tpu_custom_call" | custom-call | flops 12000000000 | bytes 25165824 | tf_op jit(solution)/shard_map/edge_block/pallas_call | solution.py:484
  59.7 0.0 copy-done.4
  59.8 0.0 copy-done.5
  59.8 0.0 copy-done.7
  59.8 0.0 copy-start.8
  59.8 1.6 %copy-done.8 = bf16[4096,256]{1,0:T(8,128)(2,1)S(1)} copy-done((bf16[4096,256]{1,0:T(8,128)(2,1)S(1)}, bf16[4096,256]{1,0:T(8,128)(2,1)}, u32[]{:S(2)}) %copy-start.8) | copy-done | bytes 2097176
  61.4 34.2 %return_rows.1 = (f32[4096,128]{1,0:T(8,128)S(1)}, f32[520,128]{1,0:T(8,128)S(1)}) custom-call(bf16[36,128,128]{2,1,0:T(8,128)(2,1)S(1)} %get-tuple-element.28.far_ref, bf16[4096,256]{1,0:T(8,128)(2,1)S(1)} %copy-done.8, f32[32,24,128]{2,1,0:T(8,128)S(1)} %get-tuple-element.30.pay_ref, s32[4,128]{1,0:T(4,128)S(1)} %bitcast.24, s32[4]{0:T(128)S(1)} %bitcast.27, ...), custom_call_target="tpu_custom_call" | custom-call | flops 5000000000 | bytes 8388608 | tf_op jit(solution)/shard_map/return_rows/pallas_call | solution.py:752
  95.6 0.5 slice_bitcast_fusion
  96.1 0.6 slice.10
  96.7 0.7 slice.9
  97.4 1.3 %copy.20 = f32[1,1,4096,128]{3,2,1,0:T(8,128)} copy(f32[1,1,4096,128]{3,2,1,0:T(8,128)S(1)} %bitcast.16) | data formatting | bytes 4194304
Async XLA Ops:
  0.6 26.0 %copy-start = (bf16[384,128]{1,0:T(8,128)(2,1)S(1)}, bf16[384,128]{1,0:T(8,128)(2,1)}, u32[]{:S(2)}) copy-start(bf16[384,128]{1,0:T(8,128)(2,1)} %w1_ref.5) | copy-start | bytes 294916
  0.6 26.0 %copy-start.1 = (s32[1,1,16384]{2,1,0:T(1,128)S(1)}, s32[1,1,16384]{2,1,0:T(1,128)}, u32[]{:S(2)}) copy-start(s32[1,1,16384]{2,1,0:T(1,128)} %param.20) | copy-start | bytes 196612
  0.7 26.0 %copy-start.2 = (s32[1,1,16384]{2,1,0:T(1,128)S(1)}, s32[1,1,16384]{2,1,0:T(1,128)}, u32[]{:S(2)}) copy-start(s32[1,1,16384]{2,1,0:T(1,128)} %param.21) | copy-start | bytes 196612
  0.7 26.0 %copy-start.3 = (bf16[128,128]{1,0:T(8,128)(2,1)S(1)}, bf16[128,128]{1,0:T(8,128)(2,1)}, u32[]{:S(2)}) copy-start(bf16[128,128]{1,0:T(8,128)(2,1)} %w2_ref.1) | copy-start | bytes 98308
  0.7 26.0 %copy-start.6 = (f32[128]{0:T(128)S(1)}, f32[128]{0:T(128)}, u32[]{:S(2)}) copy-start(f32[128]{0:T(128)} %param.16) | copy-start | bytes 1540
  26.6 1.3 %copy-start.9 = (bf16[36,128,128]{2,1,0:T(8,128)(2,1)S(1)}, bf16[36,128,128]{2,1,0:T(8,128)(2,1)}, u32[]{:S(2)}) copy-start(bf16[36,128,128]{2,1,0:T(8,128)(2,1)} %get-tuple-element.23.pr_t) | copy-start | bytes 3538948
  27.9 1.3 %copy-start.10 = (bf16[36,128,128]{2,1,0:T(8,128)(2,1)S(1)}, bf16[36,128,128]{2,1,0:T(8,128)(2,1)}, u32[]{:S(2)}) copy-start(bf16[36,128,128]{2,1,0:T(8,128)(2,1)} %get-tuple-element.24.ca_t) | copy-start | bytes 3538948
  29.2 0.7 copy-start.11
  29.9 29.9 %copy-start.4 = (s32[1,1,4,1024]{3,2,1,0:T(4,128)S(1)}, s32[1,1,4,1024]{3,2,1,0:T(4,128)}, u32[]{:S(2)}) copy-start(s32[1,1,4,1024]{3,2,1,0:T(4,128)} %param.19) | copy-start | bytes 49156
  29.9 29.9 %copy-start.5 = (s32[1,1,4,128]{3,2,1,0:T(4,128)S(1)}, s32[1,1,4,128]{3,2,1,0:T(4,128)}, u32[]{:S(2)}) copy-start(s32[1,1,4,128]{3,2,1,0:T(4,128)} %param.17) | copy-start | bytes 6148
  29.9 29.9 %copy-start.7 = (s32[1,1,4]{2,1,0:T(1,128)S(1)}, s32[1,1,4]{2,1,0:T(1,128)}, u32[]{:S(2)}) copy-start(s32[1,1,4]{2,1,0:T(1,128)} %param.18) | copy-start | bytes 52
  59.8 1.6 %copy-start.8 = (bf16[4096,256]{1,0:T(8,128)(2,1)S(1)}, bf16[4096,256]{1,0:T(8,128)(2,1)}, u32[]{:S(2)}) copy-start(bf16[4096,256]{1,0:T(8,128)(2,1)} %get-tuple-element.29.own_ref) | copy-start | bytes 6291460

commit v5 on v4

--- a/solution.py
+++ b/solution.py
@@ -438,7 +438,7 @@
             own_ref[rows, :] = both
             return 0
 
-        lax.fori_loop(0, OWN_BLOCKS // 4, own, 0, unroll=4)
+        lax.fori_loop(0, OWN_BLOCKS // 4, own, 0, unroll=8)
         _, both = owned(OWN_BLOCKS // 4)
         back = mmt(wsr, both).astype(BF16)
         for n in range(MIG_BLOCKS):
@@ -454,7 +454,7 @@
             fsr_acc[:, :TILE] += mm(tab, s)
             return 0
 
-        lax.fori_loop(0, HALO_BLOCKS // 4, halo, 0, unroll=4)
+        lax.fori_loop(0, HALO_BLOCKS // 4, halo, 0, unroll=8)
         first = fsr_acc[:, :TILE]
         second = fsr_acc[:, TILE:]
         edge_part = fe_acc[...].T
@@ -629,7 +629,7 @@
         lat_ref[rows, :] = mmt(own_buf[rows, :], wsr)
         return 0
 
-    lax.fori_loop(0, OWN_BLOCKS // 4, own_part, 0, unroll=2)
+    lax.fori_loop(0, OWN_BLOCKS // 4, own_part, 0, unroll=8)
     lax.fori_loop(1, RANKS, wait_scatter, 0)
 
     pay_copy.wait()

time: 99 us -> 99.1 us (level)
  no operation moved by 1% of the time
where the time goes in v5:
time: 99.1 us; the launch traced here: 98.8 us
  Pallas kernels  90 us (91%)
  local copies, waits for them, and re-layouts  7.98 us (8%)
    pallas_call x1, Pallas kernels, give_back(): pl.pallas_call(return_kernel, name='return_rows', out_shape=(jax.ShapeDty...  35.2 us
    pallas_call x1, Pallas kernels, edge_pass(): pl.pallas_call(edge_kernel, name='edge_block', grid_spec=pltpu.PrefetchSc...  28.9 us
    pallas_call x1, Pallas kernels, fetch(): pl.pallas_call(fetch_kernel, name='fetch_rows', out_shape=(jax.ShapeDtype...  25.9 us
    unnamed x25, local copies, waits for them, and re-layouts  6.15 us

profile of v5, /device:TPU:1, one launch (start us, length us, event | category | flops | bytes accessed | tf_op | source)
XLA Modules:
  0.0 98.8 jit_solution(477972331988480511)
XLA Ops:
  0.6 0.0 copy-start
  0.6 0.0 copy-start.1
  0.7 0.0 copy-start.2
  0.7 0.0 copy-start.3
  0.7 0.0 copy-start.6
  0.7 25.9 %fetch_rows.1 = (bf16[68,128,128]{2,1,0:T(8,128)(2,1)}, bf16[68,128,128]{2,1,0:T(8,128)(2,1)}, bf16[36,128,128]{2,1,0:T(8,128)(2,1)}, bf16[36,128,128]{2,1,0:T(8,128)(2,1)}, s32[2,128]{1,0:T(2,128)}) custom-call(bf16[4096,128]{1,0:T(8,128)(2,1)} %bitcast.31, s32[4,128]{1,0:T(4,128)} %bitcast.23, s32[4]{0:T(128)} %bitcast.26, s32[4,1024]{1,0:T(4,128)} %bitcast.21, ...), custom_call_target="tpu_custom_call" | custom-call | flops 5000000000 | bytes 8388608 | tf_op jit(solution)/shard_map/fetch_rows/pallas_call | solution.py:281
  26.6 0.0 copy-done
  26.6 0.0 copy-done.1
  26.6 0.0 copy-done.2
  26.6 0.0 copy-done.3
  26.6 0.0 copy-done.6
  26.6 0.0 copy-start.9
  26.7 1.3 %copy-done.9 = bf16[36,128,128]{2,1,0:T(8,128)(2,1)S(1)} copy-done((bf16[36,128,128]{2,1,0:T(8,128)(2,1)S(1)}, bf16[36,128,128]{2,1,0:T(8,128)(2,1)}, u32[]{:S(2)}) %copy-start.9) | copy-done | bytes 1179672
  27.9 0.0 copy-start.10
  27.9 1.3 %copy-done.10 = bf16[36,128,128]{2,1,0:T(8,128)(2,1)S(1)} copy-done((bf16[36,128,128]{2,1,0:T(8,128)(2,1)S(1)}, bf16[36,128,128]{2,1,0:T(8,128)(2,1)}, u32[]{:S(2)}) %copy-start.10) | copy-done | bytes 1179672
  29.2 0.0 copy-start.11
  29.2 0.7 copy-done.11
  29.9 0.0 copy-start.4
  29.9 0.0 copy-start.5
  29.9 0.0 copy-start.7
  29.9 28.9 %edge_block.1 = (bf16[16384,128]{1,0:T(8,128)(2,1)}, bf16[16384,128]{1,0:T(8,128)(2,1)}, bf16[4608,128]{1,0:T(8,128)(2,1)}, bf16[36,128,128]{2,1,0:T(8,128)(2,1)...) custom-call(s32[2,128]{1,0:T(2,128)S(1)} %copy-done.11, bf16[16384,128]{1,0:T(8,128)(2,1)} %bitcast.28, ...), custom_call_target="tpu_custom_call" | custom-call | flops 12000000000 | bytes 25165824 | tf_op jit(solution)/shard_map/edge_block/pallas_call | solution.py:484
  58.8 0.0 copy-done.4
  58.8 0.0 copy-done.5
  58.8 0.0 copy-done.7
  58.9 0.0 copy-start.8
  58.9 1.6 %copy-done.8 = bf16[4096,256]{1,0:T(8,128)(2,1)S(1)} copy-done((bf16[4096,256]{1,0:T(8,128)(2,1)S(1)}, bf16[4096,256]{1,0:T(8,128)(2,1)}, u32[]{:S(2)}) %copy-start.8) | copy-done | bytes 2097176
  60.5 35.2 %return_rows.1 = (f32[4096,128]{1,0:T(8,128)S(1)}, f32[520,128]{1,0:T(8,128)S(1)}) custom-call(bf16[36,128,128]{2,1,0:T(8,128)(2,1)S(1)} %get-tuple-element.28.far_ref, bf16[4096,256]{1,0:T(8,128)(2,1)S(1)} %copy-done.8, f32[32,24,128]{2,1,0:T(8,128)S(1)} %get-tuple-element.30.pay_ref, s32[4,128]{1,0:T(4,128)S(1)} %bitcast.24, s32[4]{0:T(128)S(1)} %bitcast.27, ...), custom_call_target="tpu_custom_call" | custom-call | flops 5000000000 | bytes 8388608 | tf_op jit(solution)/shard_map/return_rows/pallas_call | solution.py:752
  95.6 0.5 slice_bitcast_fusion
  96.1 0.6 slice.10
  96.8 0.7 slice.9
  97.5 1.3 %copy.20 = f32[1,1,4096,128]{3,2,1,0:T(8,128)} copy(f32[1,1,4096,128]{3,2,1,0:T(8,128)S(1)} %bitcast.16) | data formatting | bytes 4194304
Async XLA Ops:
  0.6 26.0 %copy-start = (bf16[384,128]{1,0:T(8,128)(2,1)S(1)}, bf16[384,128]{1,0:T(8,128)(2,1)}, u32[]{:S(2)}) copy-start(bf16[384,128]{1,0:T(8,128)(2,1)} %w1_ref.5) | copy-start | bytes 294916
  0.6 26.0 %copy-start.1 = (s32[1,1,16384]{2,1,0:T(1,128)S(1)}, s32[1,1,16384]{2,1,0:T(1,128)}, u32[]{:S(2)}) copy-start(s32[1,1,16384]{2,1,0:T(1,128)} %param.20) | copy-start | bytes 196612
  0.7 26.0 %copy-start.2 = (s32[1,1,16384]{2,1,0:T(1,128)S(1)}, s32[1,1,16384]{2,1,0:T(1,128)}, u32[]{:S(2)}) copy-start(s32[1,1,16384]{2,1,0:T(1,128)} %param.21) | copy-start | bytes 196612
  0.7 26.0 %copy-start.3 = (bf16[128,128]{1,0:T(8,128)(2,1)S(1)}, bf16[128,128]{1,0:T(8,128)(2,1)}, u32[]{:S(2)}) copy-start(bf16[128,128]{1,0:T(8,128)(2,1)} %w2_ref.1) | copy-start | bytes 98308
  0.7 26.0 %copy-start.6 = (f32[128]{0:T(128)S(1)}, f32[128]{0:T(128)}, u32[]{:S(2)}) copy-start(f32[128]{0:T(128)} %param.16) | copy-start | bytes 1540
  26.6 1.3 %copy-start.9 = (bf16[36,128,128]{2,1,0:T(8,128)(2,1)S(1)}, bf16[36,128,128]{2,1,0:T(8,128)(2,1)}, u32[]{:S(2)}) copy-start(bf16[36,128,128]{2,1,0:T(8,128)(2,1)} %get-tuple-element.23.pr_t) | copy-start | bytes 3538948
  27.9 1.3 %copy-start.10 = (bf16[36,128,128]{2,1,0:T(8,128)(2,1)S(1)}, bf16[36,128,128]{2,1,0:T(8,128)(2,1)}, u32[]{:S(2)}) copy-start(bf16[36,128,128]{2,1,0:T(8,128)(2,1)} %get-tuple-element.24.ca_t) | copy-start | bytes 3538948
  29.2 0.7 copy-start.11
  29.9 29.0 %copy-start.4 = (s32[1,1,4,1024]{3,2,1,0:T(4,128)S(1)}, s32[1,1,4,1024]{3,2,1,0:T(4,128)}, u32[]{:S(2)}) copy-start(s32[1,1,4,1024]{3,2,1,0:T(4,128)} %param.19) | copy-start | bytes 49156
  29.9 29.0 %copy-start.5 = (s32[1,1,4,128]{3,2,1,0:T(4,128)S(1)}, s32[1,1,4,128]{3,2,1,0:T(4,128)}, u32[]{:S(2)}) copy-start(s32[1,1,4,128]{3,2,1,0:T(4,128)} %param.17) | copy-start | bytes 6148
  29.9 29.0 %copy-start.7 = (s32[1,1,4]{2,1,0:T(1,128)S(1)}, s32[1,1,4]{2,1,0:T(1,128)}, u32[]{:S(2)}) copy-start(s32[1,1,4]{2,1,0:T(1,128)} %param.18) | copy-start | bytes 52
  58.9 1.6 %copy-start.8 = (bf16[4096,256]{1,0:T(8,128)(2,1)S(1)}, bf16[4096,256]{1,0:T(8,128)(2,1)}, u32[]{:S(2)}) copy-start(bf16[4096,256]{1,0:T(8,128)(2,1)} %get-tuple-element.29.own_ref) | copy-start | bytes 6291460
